TPU v7x, 32 devices: a whole 2x2x4 slice. The times are simulated.
32 devices in a mesh: row: 4 (over y, x), col: 8 (over z, core).
Axes of the slice: x: 2, y: 2, z: 4, core: 2. Of those that a mesh axis runs over, the one named last changes fastest.
Arguments:
- a_blocks: bfloat16 [8, 4, 16, 32, 128], P('col', 'row'), may hold values from -1 to 1
- a_scale: float32 [8, 4, 16, 4], P('col', 'row'), may hold values from 0.25 to 4
- a_cols: int32 [8, 4, 16, 4], P('col', 'row'), may hold values from 0 to 1023, as said below
- b_blocks: bfloat16 [8, 4, 1024, 32, 128], P('col', 'row'), may hold values from -1 to 1
- b_scale: float32 [8, 4, 1024, 4], P('col', 'row'), may hold values from 0.25 to 4
- b_cols: int32 [8, 4, 1024, 4], P('col', 'row'), may hold values from 0 to 511, as said below
Outputs:
- product: bfloat16 [8, 4, 8, 32, 16384], P('col', 'row')
Inputs may be any that keep to these rules, and one draw needn't show every extreme that they name: `a_cols`: the 4 columns of each block row are distinct. `b_cols`: the 4 columns of each block row are distinct.
All inputs are finite; a program needn't handle non-finite values.
Results may differ from a plain program's by a relative error of at most 0.0034.
Values may be sent and summed in bfloat16 or wider, within the bound.
No kernel may reach another device: no remote copies, remote signals or barrier semaphores. Data moves between devices by JAX's collectives and lax.ppermute only.
A program may use at most 192 MiB of HBM per device.

v0:
```python
import functools

import jax
import jax.numpy as jnp
from jax import lax
from jax.experimental import pallas as pl
from jax.experimental.pallas import tpu as pltpu
from jax.sharding import PartitionSpec as P

JW = 512
LANES = 128
META = 16
PARTS = 5
F32, BF16, I32 = jnp.float32, jnp.bfloat16, jnp.int32
VMEM_LIMIT = 12 * 1024 * 1024


def in_vmem(x):
    return pltpu.with_memory_space_constraint(x, pltpu.VMEM)


def three_parts(x):
    high = x.astype(BF16).astype(F32)
    rest = x - high
    mid = rest.astype(BF16).astype(F32)
    return [high, mid, (rest - mid).astype(BF16).astype(F32)]


def stacked(parts, rows):
    which = lax.broadcasted_iota(I32, (rows, parts[0].shape[1]), 0)
    tile = jnp.zeros(which.shape, F32)
    for at, part in enumerate(parts):
        tile = jnp.where(which == at, jnp.broadcast_to(part, which.shape), tile)
    return tile


def entries(values, first, half, rb):
    ra = values.shape[0]
    one = [values[m : m + 1, first : first + half] for m in range(ra)]
    return jnp.concatenate(one * rb, axis=1)


def gather_kernel(half, ra, rb, bs, first, pieces, cuts, *refs):
    refs = list(refs)
    take = lambda count: [refs.pop(0) for _ in range(count)]
    parity, cols_s, cols_v, b = take(4)
    if first:
        bscale, bcols = take(2)
    else:
        (table,) = take(1)
    if pieces:
        a, ascale = take(2)
    (b_same,) = take(1)
    if first:
        table, acc = take(2)
    if pieces:
        halves_of_a = take(2)
    outs = [take(len(cut)) for cut in cuts]
    wide = ra * bs
    kw = b.shape[0]
    odd = parity[0] == 1

    for flip in range(2):
        base = (parity[0] ^ flip) * half
        for out, (start, stop) in zip(outs[flip], cuts[flip]):

            def one_row(i, _, out=out, start=start, base=base):
                for m in range(ra):
                    t = cols_s[m, base + i]
                    at = pl.multiple_of(((i - start) * ra + m) * bs, bs)
                    out[pl.ds(at, bs), :] = b[t]
                return 0

            lax.fori_loop(start, stop, one_row, 0, unroll=2)

    if first:
        scale, column = bscale[...], bcols[...]
        rows = three_parts(scale) + [(column >> 8).astype(F32), (column & 255).astype(F32)]
        rows.append(jnp.zeros((table.shape[0] - PARTS * rb, kw), F32))
        table[...] = jnp.concatenate(rows, axis=0).astype(BF16)

    cols = cols_v[...]
    both = [entries(cols, h * half, half, rb) for h in range(2)]
    for flip in range(2):
        named = jnp.where(odd != (flip == 1), both[1], both[0])
        named = jnp.broadcast_to(named, (kw, named.shape[1]))
        picked = lax.broadcasted_iota(I32, named.shape, 0) == named
        picked = jnp.where(picked, 1.0, 0.0).astype(BF16)
        found = jnp.dot(table[...], picked, preferred_element_type=F32)
        slot = lax.broadcasted_iota(I32, (1, found.shape[1]), 1) // (ra * half)
        parts = []
        for part in range(PARTS):
            value = found[part * rb : part * rb + 1]
            for n in range(1, rb):
                value = jnp.where(slot == n, found[part * rb + n : part * rb + n + 1], value)
            parts.append(value)
        tile = stacked(parts, META).astype(BF16)
        for out, (start, stop) in zip(outs[flip], cuts[flip]):
            out[pl.ds((stop - start) * wide, META), :] = tile

    if pieces:
        scale = ascale[...]
        both = [entries(scale, h * half, half, rb) for h in range(2)]
        for flip, out in enumerate(halves_of_a):
            base = (parity[0] ^ flip) * half
            out[pl.ds(0, half * bs), :] = a[pl.ds(pl.multiple_of(base * bs, bs), half * bs), :]
            parts = three_parts(jnp.where(odd != (flip == 1), both[1], both[0]))
            out[pl.ds(half * bs, META), :] = stacked(parts, META).astype(BF16)

    if first:
        tiles = acc.shape[1]
        for i in range(acc.shape[0]):

            def clear(tile, _, i=i):
                acc[i, tile] = jnp.zeros(acc.shape[2:], F32)
                return 0

            lax.fori_loop(0, tiles, clear, 0, unroll=8)


def gather(parity, cols, b, half, cuts, tables=None, table=None, a=None):
    ra = cols.shape[0]
    kw, bs, width = b.shape
    rb = width // bs
    first = table is None
    smem, vmem = pl.BlockSpec(memory_space=pltpu.SMEM), pl.BlockSpec(memory_space=pltpu.VMEM)
    args = [parity, cols, cols, in_vmem(b)]
    specs = [smem, smem, vmem, vmem]
    outs = [pltpu.VMEM(b.shape, BF16)]
    if first:
        args += tables
        tiles = JW * bs // LANES
        outs.append(pltpu.VMEM((32, kw), BF16))
        outs.append(pltpu.VMEM((half, tiles, bs, LANES), F32))
    else:
        args.append(in_vmem(table))
    if a is not None:
        args += a
        outs += [pltpu.VMEM((half * bs + META, ra * bs), BF16)] * 2
    for cut in cuts:
        for start, stop in cut:
            outs.append(pltpu.VMEM(((stop - start) * ra * bs + META, width), BF16))
    specs += [vmem] * (len(args) - len(specs))
    got = pl.pallas_call(
        functools.partial(gather_kernel, half, ra, rb, bs, first, a is not None, cuts),
        out_shape=outs,
        in_specs=specs,
        out_specs=[vmem] * len(outs),
        input_output_aliases={3: 0},
        compiler_params=pltpu.CompilerParams(vmem_limit_bytes=VMEM_LIMIT),
        cost_estimate=pl.CostEstimate(flops=0, bytes_accessed=4 * 2**20, transcendentals=0),
        name="gather_rows",
    )(*args)
    got = list(got)
    messages = [[got.pop() for _ in cut][::-1] for cut in cuts[::-1]][::-1]
    return got, messages


def add_kernel(ra, rb, bs, flip, rows, flush, has_out, *refs):
    refs = list(refs)
    a, b, _ = refs.pop(0), refs.pop(0), refs.pop(0)
    if has_out:
        refs.pop(0)
    acc = refs.pop(0)
    if flush:
        target = refs.pop(0)
    prod, scl_v, col_v, scl_s, col_s, stage, sems, out_sems = refs
    first, last = rows
    wide = ra * bs
    half, tiles = acc.shape[:2]
    per = LANES // bs
    a_meta = a[flip, pl.ds(a.shape[1] - META, META), :].astype(F32)
    b_meta = b[pl.ds(b.shape[0] - META, META), :].astype(F32)
    scl_a = a_meta[0:1] + a_meta[1:2] + a_meta[2:3]
    scl_b = b_meta[0:1] + b_meta[1:2] + b_meta[2:3]
    scl_v[...] = jnp.broadcast_to(scl_a * scl_b, scl_v.shape)
    col_v[...] = jnp.broadcast_to((b_meta[3:4] * 256.0 + b_meta[4:5]).astype(I32), col_v.shape)
    moves = [
        pltpu.make_async_copy(scl_v, scl_s, sems.at[0]),
        pltpu.make_async_copy(col_v, col_s, sems.at[1]),
    ]
    for move in moves:
        move.start()
    row_block = lax.broadcasted_iota(I32, (wide, wide), 0) // bs
    col_block = lax.broadcasted_iota(I32, (wide, wide), 1) // bs
    diagonal = jnp.where(row_block == col_block, 1.0, 0.0).astype(BF16)
    for i in range(first, last):
        left = a[flip, pl.ds(i * bs, bs), :]
        left = jnp.concatenate([left] * ra, axis=0) * diagonal
        right = b[pl.ds((i - first) * wide, wide), :]
        prod[pl.ds((i - first) * wide, wide), :] = jnp.dot(left, right, preferred_element_type=F32)
    for move in moves:
        move.wait()
    lane_block = lax.broadcasted_iota(I32, (bs, LANES), 1) // bs

    def one_row(i, _):
        for m in range(ra):
            value = prod[pl.ds(pl.multiple_of(((i - first) * ra + m) * bs, bs), bs), :]
            for n in range(rb):
                entry = (n * ra + m) * half + i
                column = col_s[0, entry]
                place = column & (per - 1)
                moved = pltpu.roll(value, ((place - n) & (per - 1)) * bs, 1)
                moved = jnp.where(lane_block == place, moved * scl_s[0, entry], 0.0)
                tile = column // per
                acc[i, tile] = acc[i, tile] + moved
        return 0

    lax.fori_loop(first, last, one_row, 0)
    if flush:

        def send(i):
            slot = (i - first) % 2
            return pltpu.make_async_copy(stage.at[slot], target.at[i], out_sems.at[slot])

        for i in range(first, last):
            if i - first >= 2:
                send(i - 2).wait()
            for tile in range(tiles):
                stage[(i - first) % 2, :, pl.ds(tile * LANES, LANES)] = acc[i, tile].astype(BF16)
            send(i).start()
        for i in range(max(first, last - 2), last):
            send(i).wait()


def add_products(a, b, flip, shape, rows, acc, flush=False, out=None):
    half, ra, rb, bs = shape
    out_shapes = [pltpu.VMEM(acc.shape, F32)]
    if flush:
        out_shapes.append(jax.ShapeDtypeStruct((half, bs, JW * bs), BF16))
    vmem = pl.BlockSpec(memory_space=pltpu.VMEM)
    anywhere = pl.BlockSpec(memory_space=pl.ANY)
    args, specs = [a, b, in_vmem(acc)], [vmem] * 3
    aliases = {2: 0}
    if out is not None:
        aliases[len(args)] = 1
        args.append(out)
        specs.append(anywhere)
    count = rows[1] - rows[0]
    return pl.pallas_call(
        functools.partial(add_kernel, ra, rb, bs, flip, rows, flush, out is not None),
        out_shape=out_shapes,
        in_specs=specs,
        out_specs=[vmem, anywhere][: len(out_shapes)],
        input_output_aliases=aliases,
        scratch_shapes=[
            pltpu.VMEM((count * ra * bs, rb * bs), F32),
            pltpu.VMEM((8, LANES), F32),
            pltpu.VMEM((8, LANES), I32),
            pltpu.SMEM((8, LANES), F32),
            pltpu.SMEM((8, LANES), I32),
            pltpu.VMEM((2, bs, JW * bs) if flush else (2, 16, LANES), BF16),
            pltpu.SemaphoreType.DMA((2,)),
            pltpu.SemaphoreType.DMA((2,)),
        ],
        compiler_params=pltpu.CompilerParams(vmem_limit_bytes=VMEM_LIMIT),
        cost_estimate=pl.CostEstimate(flops=0, bytes_accessed=6 * 2**20, transcendentals=0),
        name="add_products",
    )(*args)


def on_device(a_blocks, a_scale, a_cols, b_blocks, b_scale, b_cols):
    panels = lax.axis_size("row")
    columns = lax.axis_size("col")
    halves = columns // panels
    a_part, a_scl, a_pos = a_blocks[0, 0], a_scale[0, 0].T, a_cols[0, 0].T
    b_part = b_blocks[0, 0]
    b_scl, b_pos = b_scale[0, 0].T, b_cols[0, 0].T
    nrows, bs, _ = a_part.shape
    ra, rb = a_scl.shape[0], b_scl.shape[0]
    half = nrows // halves
    shape = (half, ra, rb, bs)
    parity = (lax.axis_index("col") % halves).astype(I32).reshape(1)

    def step(value, by, flip):
        pairs = [
            (c, ((c // halves + by) % panels) * halves + (c % halves ^ flip)) for c in range(columns)
        ]
        return lax.ppermute(value, "col", pairs)

    def named_by(by):
        pairs = []
        for r in range(panels):
            for c in range(columns):
                to_row = (r + by) % panels
                to_col = (c - halves * by) % columns
                pairs.append((r * columns + c, to_row * columns + to_col))
        return lax.ppermute(a_pos, ("row", "col"), pairs)

    order = sorted(range(1, panels), key=lambda by: -min(by, panels - by))
    asked = {by: named_by(by) for by in order}
    every = (0, half)
    early = (0, half - max(1, half // 4))
    late = (early[1], half)

    messages = {}
    (b_here, table, acc), messages[0] = gather(
        parity, a_pos, b_part, half, [[every], [every]], tables=[b_scl, b_pos]
    )
    for place, by in enumerate(order):
        a = [a_part.reshape(nrows * bs, ra * bs), a_scl] if place == min(1, len(order) - 1) else None
        cuts = [[every], [early, late] if by == order[-1] else [every]]
        got, messages[by] = gather(parity, asked[by], b_here, half, cuts, table=table, a=a)
        b_here = got[0]
        if a is not None:
            kept, given = got[1:]
    left = {0: jnp.stack([kept, step(given, 0, 1)])}
    for by in order:
        pairs = [(r, (r + by) % panels) for r in range(panels)]
        left[by] = lax.ppermute(left[0], "row", pairs)

    (acc,) = add_products(kept[None], messages[0][0][0], 0, shape, every, acc)
    (acc,) = add_products(left[0], step(messages[0][1][0], 0, 1), 1, shape, every, acc)
    for by in order:
        for flip in range(halves):
            arrived = [step(message, by, flip) for message in messages[by][flip]]
            if len(arrived) == 1:
                (acc,) = add_products(left[by], arrived[0], flip, shape, every, acc)
            else:
                acc, out = add_products(left[by], arrived[0], flip, shape, early, acc, flush=True)
                _, out = add_products(left[by], arrived[1], flip, shape, late, acc, flush=True, out=out)
    return out[None, None]


def solution(mesh):
    in_specs = (
        P("col", "row", None, None, None),
        P("col", "row", None, None),
        P("col", "row", None, None),
        P("col", "row", None, None, None),
        P("col", "row", None, None),
        P("col", "row", None, None),
    )
    out_specs = P("col", "row", None, None, None)
    return jax.shard_map(
        on_device, mesh=mesh, in_specs=in_specs, out_specs=out_specs, check_vma=False
    )
```

profile of v0, /device:TPU:0, one launch (start us, length us, event | category | flops | bytes accessed | tf_op | source)
XLA Modules:
  0.0 95.4 jit_solution(3222297369005967915)
XLA Ops:
  0.0 0.0 copy-start.3
  0.0 0.0 copy-start.7
  0.0 0.0 copy-start.6
  0.0 0.0 copy-start.4
  0.0 0.0 copy-start.5
  0.0 8.3 %copy.36 = bf16[1,1,1024,32,128]{4,3,2,1,0:T(8,128)(2,1)} copy(bf16[1,1,1024,32,128]{4,3,2,1,0:T(8,128)(2,1)} %param.9) | data formatting | bytes 16777216
  8.3 0.0 copy-done.6
  8.3 5.0 %collective-permute-start.1 = (s32[4,16]{1,0:T(4,128)S(1)}, s32[4,16]{1,0:T(4,128)S(1)}, u32[]{:S(2)}, u32[]{:S(2)}) collective-permute-start(s32[4,16]{1,0:T(4,128)S(1)} %bitcast.24), channel_id=1, source_target_pairs={{0,20},{1,21},{2,22},{3,23},{4,16},{5,17},{6,18},{7,19},{8,28},{9,... | collective-permute-start | bytes 776 | tf_op jit(solution)/shard_map/ppermute | solution.py:288
  13.3 2.3 %collective-permute-start = (s32[4,16]{1,0:T(4,128)S(1)}, s32[4,16]{1,0:T(4,128)S(1)}, u32[]{:S(2)}, u32[]{:S(2)}) collective-permute-start(s32[4,16]{1,0:T(4,128)S(1)} %bitcast.25), channel_id=1, source_target_pairs={{0,14},{1,15},{2,8},{3,9},{4,10},{5,11},{6,12},{7,13},{8,22},{9,23... | collective-permute-start | bytes 776 | tf_op jit(solution)/shard_map/ppermute | solution.py:288
  15.6 0.0 copy-done.4
  15.6 0.0 copy-done.5
  15.6 0.0 copy-start
  15.6 3.4 %copy-done = bf16[1,1,1024,32,128]{4,3,2,1,0:T(8,128)(2,1)S(1)} copy-done((bf16[1,1,1024,32,128]{4,3,2,1,0:T(8,128)(2,1)S(1)}, bf16[1,1,1024,32,128]{4,3,2,1,0:T(8,128)(2,1)}, u32[]{:S(2)}) %copy-start) | copy-done | bytes 8388632
  19.0 2.8 %gather_rows.4 = (bf16[1024,32,128]{2,1,0:T(8,128)(2,1)S(1)}, bf16[32,1024]{1,0:T(8,128)(2,1)S(1)}, f32[8,128,32,128]{3,2,1,0:T(8,128)S(1)}, bf16[1040,128]{1,0:T(8,128)(2,1)S(1)}, bf16[1040,128]{1,0:T(8,128)(2,1)S(1)}) custom-call(s32[1]{0:T(128)} %bitcast.refs_0_, s32[4,16]{1,0:T(4,128)S(1)} %bitcast.26, ...), custom_call_target="tpu_custom_call", output_to_operand_aliasing={{0}: (3, {})} | custom-call | bytes 4194304 | tf_op jit(solution)/shard_map/gather_rows/pallas_call | solution.py:144
  21.7 0.0 copy-start.1
  21.8 3.4 %copy-done.1 = bf16[1024,32,128]{2,1,0:T(8,128)(2,1)} copy-done((bf16[1024,32,128]{2,1,0:T(8,128)(2,1)}, bf16[1024,32,128]{2,1,0:T(8,128)(2,1)S(1)}, u32[]{:S(2)}) %copy-start.1) | copy-done | bytes 8388632
  25.1 0.0 collective-permute-done.1.refs_1_.refs_2_
  25.2 0.0 copy-start.2
  25.2 3.4 %copy-done.2 = bf16[1024,32,128]{2,1,0:T(8,128)(2,1)S(1)} copy-done((bf16[1024,32,128]{2,1,0:T(8,128)(2,1)S(1)}, bf16[1024,32,128]{2,1,0:T(8,128)(2,1)}, u32[]{:S(2)}) %copy-start.2) | copy-done | bytes 8388632
  28.5 1.2 %gather_rows.5 = (bf16[1024,32,128]{2,1,0:T(8,128)(2,1)S(1)}, bf16[1040,128]{1,0:T(8,128)(2,1)S(1)}, bf16[1040,128]{1,0:T(8,128)(2,1)S(1)}) custom-call(s32[1]{0:T(128)} %bitcast.refs_0_, s32[4,16]{1,0:T(4,128)S(1)} %collective-permute-done.1.refs_1_.refs_2_, s32[4,16]{1,0:T(4,128)S(1)} %collective-permute-done.1.refs_1_.refs_2_, ...), custom_call_target="tpu_custom_call", output_to_operand_aliasing={{0}: (3, {})} | custom-call | bytes 4194304 | tf_op jit(solution)/shard_map/gather_rows/pallas_call | solution.py:144
  29.7 0.0 collective-permute-done.refs_1_.refs_2_
  29.8 0.0 copy-done.3
  29.8 0.0 copy-done.7
  29.8 1.2 %gather_rows.6 = (bf16[1024,32,128]{2,1,0:T(8,128)(2,1)S(1)}, bf16[272,128]{1,0:T(8,128)(2,1)S(1)}, bf16[272,128]{1,0:T(8,128)(2,1)S(1)}, bf16[1040,128]{1,0:T(8,128)(2,1)S(1)}, bf16[1040,128]{1,0:T(8,128)(2,1)S(1)}) custom-call(s32[1]{0:T(128)} %bitcast.refs_0_, s32[4,16]{1,0:T(4,128)S(1)} %collective-permute-done.refs_1_.refs_2_, ...), custom_call_target="tpu_custom_call", output_to_operand_aliasing={{0}: (3, {})} | custom-call | bytes 4194304 | tf_op jit(solution)/shard_map/gather_rows/pallas_call | solution.py:144
  31.0 0.1 collective-permute-start.2
  31.1 0.5 collective-permute-start.14
  31.6 0.7 collective-permute-done.2
  32.3 0.6 collective-permute-start.11
  32.9 1.2 %collective-permute-start.12 = (bf16[1040,128]{1,0:T(8,128)(2,1)S(1)}, bf16[1040,128]{1,0:T(8,128)(2,1)S(1)}, u32[]{:S(2)}, u32[]{:S(2)}) collective-permute-start(bf16[1040,128]{1,0:T(8,128)(2,1)S(1)} %get-tuple-element.35), channel_id=1, source_target_pairs={{0,5},{1,4},{2,7},{3,6},{4,1},{5,0},{6,3},{7,2},{8,13},{9,12},{10,... | collective-permute-start | bytes 798728 | tf_op jit(solution)/shard_map/ppermute | solution.py:279
  34.1 0.4 collective-permute-start.4
  34.5 1.1 %collective-permute-start.8 = (bf16[2,272,128]{2,1,0:T(8,128)(2,1)S(1)}, bf16[2,272,128]{2,1,0:T(8,128)(2,1)S(1)}, u32[]{:S(2)}, u32[]{:S(2)}) collective-permute-start(bf16[2,272,128]{2,1,0:T(8,128)(2,1)S(1)} %pad_maximum_fusion.refs_0_), channel_id=1, source_target_pairs={{0,8},{8,16},{16,24},{24,0},{1,9},{9,17},{17,25},{25,1},{2,10},{10... | collective-permute-start | bytes 417800 | tf_op jit(solution)/shard_map/ppermute | solution.py:310
  35.6 8.1 %collective-permute-done.4.refs_1_.refs_2_ = s32[4,16]{1,0:T(4,128)S(1)} collective-permute-done((s32[4,16]{1,0:T(4,128)S(1)}, s32[4,16]{1,0:T(4,128)S(1)}, u32[]{:S(2)}, u32[]{:S(2)}) %collective-permute-start.4) | collective-permute-done | bytes 288 | tf_op jit(solution)/shard_map/ppermute | solution.py:288
  43.7 5.0 %collective-permute-start.13 = (bf16[1040,128]{1,0:T(8,128)(2,1)S(1)}, bf16[1040,128]{1,0:T(8,128)(2,1)S(1)}, u32[]{:S(2)}, u32[]{:S(2)}) collective-permute-start(bf16[1040,128]{1,0:T(8,128)(2,1)S(1)} %get-tuple-element.36), channel_id=1, source_target_pairs={{0,4},{1,5},{2,6},{3,7},{4,0},{5,1},{6,2},{7,3},{8,12},{9,13},{10,... | collective-permute-start | bytes 798728 | tf_op jit(solution)/shard_map/ppermute | solution.py:279
  48.7 0.0 collective-permute-done.11.refs_0_
  48.7 0.0 collective-permute-start.10
  48.7 1.2 %gather_rows.7 = (bf16[1024,32,128]{2,1,0:T(8,128)(2,1)S(1)}, bf16[1040,128]{1,0:T(8,128)(2,1)S(1)}, bf16[784,128]{1,0:T(8,128)(2,1)S(1)}, bf16[272,128]{1,0:T(8,128)(2,1)S(1)}) custom-call(s32[1]{0:T(128)} %bitcast.refs_0_, s32[4,16]{1,0:T(4,128)S(1)} %collective-permute-done.4.refs_1_.refs_2_, ...), custom_call_target="tpu_custom_call", output_to_operand_aliasing={{0}: (3, {})} | custom-call | bytes 4194304 | tf_op jit(solution)/shard_map/gather_rows/pallas_call | solution.py:144
  49.9 0.0 collective-permute-done.8.refs_0_
  49.9 0.1 collective-permute-start.9
  50.0 0.0 collective-permute-done.14.refs_1_
  50.0 3.9 %collective-permute-start.7 = (bf16[1040,128]{1,0:T(8,128)(2,1)S(1)}, bf16[1040,128]{1,0:T(8,128)(2,1)S(1)}, u32[]{:S(2)}, u32[]{:S(2)}) collective-permute-start(bf16[1040,128]{1,0:T(8,128)(2,1)S(1)} %get-tuple-element.32), channel_id=1, source_target_pairs={{0,6},{1,7},{2,0},{3,1},{4,2},{5,3},{6,4},{7,5},{8,14},{9,15},{10,... | collective-permute-start | bytes 798728 | tf_op jit(solution)/shard_map/ppermute | solution.py:279
  53.9 0.0 collective-permute-done.12.refs_1_
  53.9 1.4 %collective-permute-start.6 = (bf16[784,128]{1,0:T(8,128)(2,1)S(1)}, bf16[784,128]{1,0:T(8,128)(2,1)S(1)}, u32[]{:S(2)}, u32[]{:S(2)}) collective-permute-start(bf16[784,128]{1,0:T(8,128)(2,1)S(1)} %get-tuple-element.31), channel_id=1, source_target_pairs={{0,7},{1,6},{2,1},{3,0},{4,3},{5,2},{6,5},{7,4},{8,15},{9,14},{10,... | collective-permute-start | bytes 602120 | tf_op jit(solution)/shard_map/ppermute | solution.py:279
  55.3 16.4 %collective-permute-done.13.refs_1_ = bf16[1040,128]{1,0:T(8,128)(2,1)S(1)} collective-permute-done((bf16[1040,128]{1,0:T(8,128)(2,1)S(1)}, bf16[1040,128]{1,0:T(8,128)(2,1)S(1)}, u32[]{:S(2)}, u32[]{:S(2)}) %collective-permute-start.13) | collective-permute-done | bytes 266272 | tf_op jit(solution)/shard_map/ppermute | solution.py:279
  71.6 1.0 %collective-permute-start.3 = (bf16[2,272,128]{2,1,0:T(8,128)(2,1)S(1)}, bf16[2,272,128]{2,1,0:T(8,128)(2,1)S(1)}, u32[]{:S(2)}, u32[]{:S(2)}) collective-permute-start(bf16[2,272,128]{2,1,0:T(8,128)(2,1)S(1)} %pad_maximum_fusion.refs_0_), channel_id=1, source_target_pairs={{0,24},{8,0},{16,8},{24,16},{1,25},{9,1},{17,9},{25,17},{2,26},{10... | collective-permute-start | bytes 417800 | tf_op jit(solution)/shard_map/ppermute | solution.py:310
  72.6 0.0 collective-permute-done.10.refs_1_
  72.6 0.0 collective-permute-start.5
  72.6 2.1 %add_products.9.refs_2_ = f32[8,128,32,128]{3,2,1,0:T(8,128)S(1)} custom-call(bf16[1,272,128]{2,1,0:T(8,128)(2,1)S(1)} %bitcast.20, bf16[1040,128]{1,0:T(8,128)(2,1)S(1)} %get-tuple-element.38.refs_1_, f32[8,128,32,128]{3,2,1,0:T(8,128)S(1)} %get-tuple-element.39.refs_2_), custom_call_target="tpu_custom_call", output_to_operand_aliasing={{}: (2, {})} | custom-call | bytes 6291456 | tf_op jit(solution)/shard_map/add_products/pallas_call | solution.py:240
  74.7 2.1 %add_products.10.refs_2_ = f32[8,128,32,128]{3,2,1,0:T(8,128)S(1)} custom-call(bf16[2,272,128]{2,1,0:T(8,128)(2,1)S(1)} %pad_maximum_fusion.refs_0_, bf16[1040,128]{1,0:T(8,128)(2,1)S(1)} %collective-permute-done.14.refs_1_, f32[8,128,32,128]{3,2,1,0:T(8,128)S(1)} %add_products.9.refs_2_), custom_call_target="tpu_custom_call", output_to_operand_aliasing={{}: (2, {})} | custom-call | bytes 6291456 | tf_op jit(solution)/shard_map/add_products/pallas_call | solution.py:240
  76.9 2.1 %add_products.11.refs_2_ = f32[8,128,32,128]{3,2,1,0:T(8,128)S(1)} custom-call(bf16[2,272,128]{2,1,0:T(8,128)(2,1)S(1)} %collective-permute-done.11.refs_0_, bf16[1040,128]{1,0:T(8,128)(2,1)S(1)} %collective-permute-done.13.refs_1_, f32[8,128,32,128]{3,2,1,0:T(8,128)S(1)} %add_products.10.refs_2_), custom_call_target="tpu_custom_call", output_to_operand_aliasing={{}: (2, {})} | custom-call | bytes 6291456 | tf_op jit(solution)/shard_map/add_products/pallas_call | solution.py:240
  79.0 2.1 %add_products.12.refs_2_ = f32[8,128,32,128]{3,2,1,0:T(8,128)S(1)} custom-call(bf16[2,272,128]{2,1,0:T(8,128)(2,1)S(1)} %collective-permute-done.11.refs_0_, bf16[1040,128]{1,0:T(8,128)(2,1)S(1)} %collective-permute-done.12.refs_1_, f32[8,128,32,128]{3,2,1,0:T(8,128)S(1)} %add_products.11.refs_2_), custom_call_target="tpu_custom_call", output_to_operand_aliasing={{}: (2, {})} | custom-call | bytes 6291456 | tf_op jit(solution)/shard_map/add_products/pallas_call | solution.py:240
  81.1 2.1 %add_products.13.refs_2_ = f32[8,128,32,128]{3,2,1,0:T(8,128)S(1)} custom-call(bf16[2,272,128]{2,1,0:T(8,128)(2,1)S(1)} %collective-permute-done.8.refs_0_, bf16[1040,128]{1,0:T(8,128)(2,1)S(1)} %collective-permute-done.10.refs_1_, f32[8,128,32,128]{3,2,1,0:T(8,128)S(1)} %add_products.12.refs_2_), custom_call_target="tpu_custom_call", output_to_operand_aliasing={{}: (2, {})} | custom-call | bytes 6291456 | tf_op jit(solution)/shard_map/add_products/pallas_call | solution.py:240
  83.2 0.0 collective-permute-done.9.refs_1_
  83.2 2.1 %add_products.14.refs_2_ = f32[8,128,32,128]{3,2,1,0:T(8,128)S(1)} custom-call(bf16[2,272,128]{2,1,0:T(8,128)(2,1)S(1)} %collective-permute-done.8.refs_0_, bf16[1040,128]{1,0:T(8,128)(2,1)S(1)} %collective-permute-done.9.refs_1_, f32[8,128,32,128]{3,2,1,0:T(8,128)S(1)} %add_products.13.refs_2_), custom_call_target="tpu_custom_call", output_to_operand_aliasing={{}: (2, {})} | custom-call | bytes 6291456 | tf_op jit(solution)/shard_map/add_products/pallas_call | solution.py:240
  85.4 0.0 collective-permute-done.3.refs_0_
  85.4 0.0 collective-permute-done.7.refs_1_
  85.4 2.1 %add_products.15.refs_2_ = f32[8,128,32,128]{3,2,1,0:T(8,128)S(1)} custom-call(bf16[2,272,128]{2,1,0:T(8,128)(2,1)S(1)} %collective-permute-done.3.refs_0_, bf16[1040,128]{1,0:T(8,128)(2,1)S(1)} %collective-permute-done.7.refs_1_, f32[8,128,32,128]{3,2,1,0:T(8,128)S(1)} %add_products.14.refs_2_), custom_call_target="tpu_custom_call", output_to_operand_aliasing={{}: (2, {})} | custom-call | bytes 6291456 | tf_op jit(solution)/shard_map/add_products/pallas_call | solution.py:240
  87.5 0.0 collective-permute-done.6.refs_1_
  87.5 5.4 %add_products.16 = (f32[8,128,32,128]{3,2,1,0:T(8,128)S(1)}, bf16[8,32,16384]{2,1,0:T(8,128)(2,1)}) custom-call(bf16[2,272,128]{2,1,0:T(8,128)(2,1)S(1)} %collective-permute-done.3.refs_0_, bf16[784,128]{1,0:T(8,128)(2,1)S(1)} %collective-permute-done.6.refs_1_, f32[8,128,32,128]{3,2,1,0:T(8,128)S(1)} %add_products.15.refs_2_), custom_call_target="tpu_custom_call", output_to_operand_aliasing={{0}: (2, {})} | custom-call | bytes 6291456 | tf_op jit(solution)/shard_map/add_products/pallas_call | solution.py:240
  92.9 0.0 collective-permute-done.5.refs_1_
  92.9 2.5 %add_products.17 = (f32[8,128,32,128]{3,2,1,0:T(8,128)S(1)}, bf16[8,32,16384]{2,1,0:T(8,128)(2,1)}) custom-call(bf16[2,272,128]{2,1,0:T(8,128)(2,1)S(1)} %collective-permute-done.3.refs_0_, bf16[272,128]{1,0:T(8,128)(2,1)S(1)} %collective-permute-done.5.refs_1_, ...), custom_call_target="tpu_custom_call", output_to_operand_aliasing={{0}: (2, {}), {1}: (3, {})} | custom-call | bytes 6291456 | tf_op jit(solution)/shard_map/add_products/pallas_call | solution.py:240
  (1 shorter events, 0.0 us)
Async XLA Ops:
  0.0 29.8 %copy-start.3 = (bf16[1,1,16,32,128]{4,3,2,1,0:T(8,128)(2,1)S(1)}, bf16[1,1,16,32,128]{4,3,2,1,0:T(8,128)(2,1)}, u32[]{:S(2)}) copy-start(bf16[1,1,16,32,128]{4,3,2,1,0:T(8,128)(2,1)} %param.6) | copy-start | bytes 393220
  0.0 29.8 %copy-start.7 = (f32[1,1,16,4]{2,3,1,0:T(4,128)S(1)}, f32[1,1,16,4]{2,3,1,0:T(4,128)}, u32[]{:S(2)}) copy-start(f32[1,1,16,4]{2,3,1,0:T(4,128)} %param.7) | copy-start | bytes 772
  0.0 8.3 %copy-start.6 = (s32[1,1,16,4]{2,3,1,0:T(4,128)S(1)}, s32[1,1,16,4]{2,3,1,0:T(4,128)}, u32[]{:S(2)}) copy-start(s32[1,1,16,4]{2,3,1,0:T(4,128)} %param.8) | copy-start | bytes 772
  0.0 15.6 %copy-start.4 = (f32[1,1,1024,4]{2,3,1,0:T(4,128)S(1)}, f32[1,1,1024,4]{2,3,1,0:T(4,128)}, u32[]{:S(2)}) copy-start(f32[1,1,1024,4]{2,3,1,0:T(4,128)} %param.10) | copy-start | bytes 49156
  0.0 15.6 %copy-start.5 = (s32[1,1,1024,4]{2,3,1,0:T(4,128)S(1)}, s32[1,1,1024,4]{2,3,1,0:T(4,128)}, u32[]{:S(2)}) copy-start(s32[1,1,1024,4]{2,3,1,0:T(4,128)} %param.11) | copy-start | bytes 49156
  8.3 16.9 %collective-permute-start.1 = (s32[4,16]{1,0:T(4,128)S(1)}, s32[4,16]{1,0:T(4,128)S(1)}, u32[]{:S(2)}, u32[]{:S(2)}) collective-permute-start(s32[4,16]{1,0:T(4,128)S(1)} %bitcast.24), channel_id=1, source_target_pairs={{0,20},{1,21},{2,22},{3,23},{4,16},{5,17},{6,18},{7,19},{8,28},{9,... | collective-permute-start | bytes 776 | tf_op jit(solution)/shard_map/ppermute | solution.py:288
  13.3 16.4 %collective-permute-start = (s32[4,16]{1,0:T(4,128)S(1)}, s32[4,16]{1,0:T(4,128)S(1)}, u32[]{:S(2)}, u32[]{:S(2)}) collective-permute-start(s32[4,16]{1,0:T(4,128)S(1)} %bitcast.25), channel_id=1, source_target_pairs={{0,14},{1,15},{2,8},{3,9},{4,10},{5,11},{6,12},{7,13},{8,22},{9,23... | collective-permute-start | bytes 776 | tf_op jit(solution)/shard_map/ppermute | solution.py:288
  15.6 3.4 %copy-start = (bf16[1,1,1024,32,128]{4,3,2,1,0:T(8,128)(2,1)S(1)}, bf16[1,1,1024,32,128]{4,3,2,1,0:T(8,128)(2,1)}, u32[]{:S(2)}) copy-start(bf16[1,1,1024,32,128]{4,3,2,1,0:T(8,128)(2,1)} %copy.36) | copy-start | bytes 25165828
  21.7 3.4 %copy-start.1 = (bf16[1024,32,128]{2,1,0:T(8,128)(2,1)}, bf16[1024,32,128]{2,1,0:T(8,128)(2,1)S(1)}, u32[]{:S(2)}) copy-start(bf16[1024,32,128]{2,1,0:T(8,128)(2,1)S(1)} %get-tuple-element.24.refs_3_) | copy-start | bytes 25165828
  25.2 3.4 %copy-start.2 = (bf16[1024,32,128]{2,1,0:T(8,128)(2,1)S(1)}, bf16[1024,32,128]{2,1,0:T(8,128)(2,1)}, u32[]{:S(2)}) copy-start(bf16[1024,32,128]{2,1,0:T(8,128)(2,1)} %copy-done.1) | copy-start | bytes 25165828
  31.0 1.3 %collective-permute-start.2 = (bf16[272,128]{1,0:T(8,128)(2,1)S(1)}, bf16[272,128]{1,0:T(8,128)(2,1)S(1)}, u32[]{:S(2)}, u32[]{:S(2)}) collective-permute-start(bf16[272,128]{1,0:T(8,128)(2,1)S(1)} %get-tuple-element.28), channel_id=1, source_target_pairs={{0,1},{1,0},{2,3},{3,2},{4,5},{5,4},{6,7},{7,6},{8,9},{9,8},{10,11... | collective-permute-start | bytes 208904 | tf_op jit(solution)/shard_map/ppermute | solution.py:279
  31.1 18.9 %collective-permute-start.14 = (bf16[1040,128]{1,0:T(8,128)(2,1)S(1)}, bf16[1040,128]{1,0:T(8,128)(2,1)S(1)}, u32[]{:S(2)}, u32[]{:S(2)}) collective-permute-start(bf16[1040,128]{1,0:T(8,128)(2,1)S(1)} %get-tuple-element.37), channel_id=1, source_target_pairs={{0,1},{1,0},{2,3},{3,2},{4,5},{5,4},{6,7},{7,6},{8,9},{9,8},{10,11... | collective-permute-start | bytes 798728 | tf_op jit(solution)/shard_map/ppermute | solution.py:279
  32.3 16.4 %collective-permute-start.11 = (bf16[2,272,128]{2,1,0:T(8,128)(2,1)S(1)}, bf16[2,272,128]{2,1,0:T(8,128)(2,1)S(1)}, u32[]{:S(2)}, u32[]{:S(2)}) collective-permute-start(bf16[2,272,128]{2,1,0:T(8,128)(2,1)S(1)} %pad_maximum_fusion.refs_0_), channel_id=1, source_target_pairs={{0,16},{8,24},{16,0},{24,8},{1,17},{9,25},{17,1},{25,9},{2,18},{10... | collective-permute-start | bytes 417800 | tf_op jit(solution)/shard_map/ppermute | solution.py:310
  32.9 21.0 %collective-permute-start.12 = (bf16[1040,128]{1,0:T(8,128)(2,1)S(1)}, bf16[1040,128]{1,0:T(8,128)(2,1)S(1)}, u32[]{:S(2)}, u32[]{:S(2)}) collective-permute-start(bf16[1040,128]{1,0:T(8,128)(2,1)S(1)} %get-tuple-element.35), channel_id=1, source_target_pairs={{0,5},{1,4},{2,7},{3,6},{4,1},{5,0},{6,3},{7,2},{8,13},{9,12},{10,... | collective-permute-start | bytes 798728 | tf_op jit(solution)/shard_map/ppermute | solution.py:279
  34.1 9.6 %collective-permute-start.4 = (s32[4,16]{1,0:T(4,128)S(1)}, s32[4,16]{1,0:T(4,128)S(1)}, u32[]{:S(2)}, u32[]{:S(2)}) collective-permute-start(s32[4,16]{1,0:T(4,128)S(1)} %bitcast.28), channel_id=1, source_target_pairs={{0,26},{1,27},{2,28},{3,29},{4,30},{5,31},{6,24},{7,25},{8,2},{9,3... | collective-permute-start | bytes 776 | tf_op jit(solution)/shard_map/ppermute | solution.py:288
  34.5 15.5 %collective-permute-start.8 = (bf16[2,272,128]{2,1,0:T(8,128)(2,1)S(1)}, bf16[2,272,128]{2,1,0:T(8,128)(2,1)S(1)}, u32[]{:S(2)}, u32[]{:S(2)}) collective-permute-start(bf16[2,272,128]{2,1,0:T(8,128)(2,1)S(1)} %pad_maximum_fusion.refs_0_), channel_id=1, source_target_pairs={{0,8},{8,16},{16,24},{24,0},{1,9},{9,17},{17,25},{25,1},{2,10},{10... | collective-permute-start | bytes 417800 | tf_op jit(solution)/shard_map/ppermute | solution.py:310
  43.7 28.0 %collective-permute-start.13 = (bf16[1040,128]{1,0:T(8,128)(2,1)S(1)}, bf16[1040,128]{1,0:T(8,128)(2,1)S(1)}, u32[]{:S(2)}, u32[]{:S(2)}) collective-permute-start(bf16[1040,128]{1,0:T(8,128)(2,1)S(1)} %get-tuple-element.36), channel_id=1, source_target_pairs={{0,4},{1,5},{2,6},{3,7},{4,0},{5,1},{6,2},{7,3},{8,12},{9,13},{10,... | collective-permute-start | bytes 798728 | tf_op jit(solution)/shard_map/ppermute | solution.py:279
  48.7 23.9 %collective-permute-start.10 = (bf16[1040,128]{1,0:T(8,128)(2,1)S(1)}, bf16[1040,128]{1,0:T(8,128)(2,1)S(1)}, u32[]{:S(2)}, u32[]{:S(2)}) collective-permute-start(bf16[1040,128]{1,0:T(8,128)(2,1)S(1)} %get-tuple-element.34), channel_id=1, source_target_pairs={{0,2},{1,3},{2,4},{3,5},{4,6},{5,7},{6,0},{7,1},{8,10},{9,11},{10,... | collective-permute-start | bytes 798728 | tf_op jit(solution)/shard_map/ppermute | solution.py:279
  49.9 33.3 %collective-permute-start.9 = (bf16[1040,128]{1,0:T(8,128)(2,1)S(1)}, bf16[1040,128]{1,0:T(8,128)(2,1)S(1)}, u32[]{:S(2)}, u32[]{:S(2)}) collective-permute-start(bf16[1040,128]{1,0:T(8,128)(2,1)S(1)} %get-tuple-element.33), channel_id=1, source_target_pairs={{0,3},{1,2},{2,5},{3,4},{4,7},{5,6},{6,1},{7,0},{8,11},{9,10},{10,... | collective-permute-start | bytes 798728 | tf_op jit(solution)/shard_map/ppermute | solution.py:279
  50.0 35.4 %collective-permute-start.7 = (bf16[1040,128]{1,0:T(8,128)(2,1)S(1)}, bf16[1040,128]{1,0:T(8,128)(2,1)S(1)}, u32[]{:S(2)}, u32[]{:S(2)}) collective-permute-start(bf16[1040,128]{1,0:T(8,128)(2,1)S(1)} %get-tuple-element.32), channel_id=1, source_target_pairs={{0,6},{1,7},{2,0},{3,1},{4,2},{5,3},{6,4},{7,5},{8,14},{9,15},{10,... | collective-permute-start | bytes 798728 | tf_op jit(solution)/shard_map/ppermute | solution.py:279
  53.9 33.6 %collective-permute-start.6 = (bf16[784,128]{1,0:T(8,128)(2,1)S(1)}, bf16[784,128]{1,0:T(8,128)(2,1)S(1)}, u32[]{:S(2)}, u32[]{:S(2)}) collective-permute-start(bf16[784,128]{1,0:T(8,128)(2,1)S(1)} %get-tuple-element.31), channel_id=1, source_target_pairs={{0,7},{1,6},{2,1},{3,0},{4,3},{5,2},{6,5},{7,4},{8,15},{9,14},{10,... | collective-permute-start | bytes 602120 | tf_op jit(solution)/shard_map/ppermute | solution.py:279
  71.6 13.7 %collective-permute-start.3 = (bf16[2,272,128]{2,1,0:T(8,128)(2,1)S(1)}, bf16[2,272,128]{2,1,0:T(8,128)(2,1)S(1)}, u32[]{:S(2)}, u32[]{:S(2)}) collective-permute-start(bf16[2,272,128]{2,1,0:T(8,128)(2,1)S(1)} %pad_maximum_fusion.refs_0_), channel_id=1, source_target_pairs={{0,24},{8,0},{16,8},{24,16},{1,25},{9,1},{17,9},{25,17},{2,26},{10... | collective-permute-start | bytes 417800 | tf_op jit(solution)/shard_map/ppermute | solution.py:310
  72.6 20.3 %collective-permute-start.5 = (bf16[272,128]{1,0:T(8,128)(2,1)S(1)}, bf16[272,128]{1,0:T(8,128)(2,1)S(1)}, u32[]{:S(2)}, u32[]{:S(2)}) collective-permute-start(bf16[272,128]{1,0:T(8,128)(2,1)S(1)} %get-tuple-element.30), channel_id=1, source_target_pairs={{0,7},{1,6},{2,1},{3,0},{4,3},{5,2},{6,5},{7,4},{8,15},{9,14},{10,... | collective-permute-start | bytes 208904 | tf_op jit(solution)/shard_map/ppermute | solution.py:279
where the time goes:
time: 95.6 us; the launch traced here: 95.4 us
  Pallas kernels  29.1 us (30%)
  waiting for transfers between devices  25.3 us (26%)
  starting transfers between devices  22.5 us (24%)
  local copies, waits for them, and re-layouts  18.4 us (19%)
    pallas_call x9, Pallas kernels, add_products(): pl.pallas_call(functools.partial(add_kernel, ra, rb, bs, flip, rows, flus...  22.7 us
    unnamed x17, local copies, waits for them, and re-layouts  18.4 us
    ppermute x9, waiting for transfers between devices, step(): return lax.ppermute(value, 'col', pairs)  17.1 us
    ppermute x9, starting transfers between devices, step(): return lax.ppermute(value, 'col', pairs)  12.1 us
    ppermute x3, waiting for transfers between devices, named_by(): return lax.ppermute(a_pos, ('row', 'col'), pairs)  8.12 us
    ppermute x3, starting transfers between devices, named_by(): return lax.ppermute(a_pos, ('row', 'col'), pairs)  7.7 us
    pallas_call x4, Pallas kernels, gather(): pl.pallas_call(functools.partial(gather_kernel, half, ra, rb, bs, first,...  6.35 us
    ppermute x3, starting transfers between devices, on_device(): left[by] = lax.ppermute(left[0], 'row', pairs)  2.66 us
  transfers between devices with their start and end apart: 15, of which 3 were waited for; matrix products, arithmetic and copies ran while one was open for 0% of the time, Pallas kernels for 27%

commit v1 on v0

--- a/solution.py
+++ b/solution.py
@@ -40,44 +40,85 @@
     return jnp.concatenate(one * rb, axis=1)
 
 
-def gather_kernel(half, ra, rb, bs, first, pieces, cuts, *refs):
-    refs = list(refs)
-    take = lambda count: [refs.pop(0) for _ in range(count)]
-    parity, cols_s, cols_v, b = take(4)
-    if first:
-        bscale, bcols = take(2)
-    else:
-        (table,) = take(1)
-    if pieces:
-        a, ascale = take(2)
-    (b_same,) = take(1)
-    if first:
-        table, acc = take(2)
-    if pieces:
-        halves_of_a = take(2)
-    outs = [take(len(cut)) for cut in cuts]
+def prepare_kernel(rb, bscale, bcols, table, acc):
+    scale, column = bscale[...], bcols[...]
+    rows = three_parts(scale) + [(column >> 8).astype(F32), (column & 255).astype(F32)]
+    rows.append(jnp.zeros((table.shape[0] - PARTS * rb, table.shape[1]), F32))
+    table[...] = jnp.concatenate(rows, axis=0).astype(BF16)
+    for i in range(acc.shape[0]):
+
+        def clear(tile, _, i=i):
+            acc[i, tile] = jnp.zeros(acc.shape[2:], F32)
+            return 0
+
+        lax.fori_loop(0, acc.shape[1], clear, 0, unroll=8)
+
+
+def prepare(bscale, bcols, half, bs):
+    rb, kw = bscale.shape
+    vmem = pl.BlockSpec(memory_space=pltpu.VMEM)
+    return pl.pallas_call(
+        functools.partial(prepare_kernel, rb),
+        out_shape=[
+            pltpu.VMEM((-(-PARTS * rb // 16) * 16, kw), BF16),
+            pltpu.VMEM((half, JW * bs // LANES, bs, LANES), F32),
+        ],
+        in_specs=[vmem] * 2,
+        out_specs=[vmem] * 2,
+        compiler_params=pltpu.CompilerParams(vmem_limit_bytes=VMEM_LIMIT),
+        cost_estimate=pl.CostEstimate(flops=0, bytes_accessed=8 * 2**20, transcendentals=0),
+        name="prepare",
+    )(bscale, bcols)
+
+
+def split_kernel(half, rb, bs, parity, a, ascale, after, kept, given):
+    scale = ascale[...]
+    both = [entries(scale, h * half, half, rb) for h in range(2)]
+    odd = parity[0] == 1
+    for flip, out in enumerate((kept, given)):
+        base = (parity[0] ^ flip) * half
+        out[pl.ds(0, half * bs), :] = a[pl.ds(pl.multiple_of(base * bs, bs), half * bs), :]
+        parts = three_parts(jnp.where(odd != (flip == 1), both[1], both[0]))
+        out[pl.ds(half * bs, META), :] = stacked(parts, META).astype(BF16)
+
+
+def split(parity, a, ascale, half, rb, bs, after):
+    smem, vmem = pl.BlockSpec(memory_space=pltpu.SMEM), pl.BlockSpec(memory_space=pltpu.VMEM)
+    return pl.pallas_call(
+        functools.partial(split_kernel, half, rb, bs),
+        out_shape=[pltpu.VMEM((half * bs + META, a.shape[1]), BF16)] * 2,
+        in_specs=[smem, vmem, vmem, pl.BlockSpec(memory_space=pl.ANY)],
+        out_specs=[vmem] * 2,
+        compiler_params=pltpu.CompilerParams(vmem_limit_bytes=VMEM_LIMIT),
+        cost_estimate=pl.CostEstimate(flops=0, bytes_accessed=1024, transcendentals=0),
+        name="split",
+    )(parity, a, ascale, after)
+
+
+def gather_kernel(half, ra, rb, bs, cuts, afters, parity, cols_s, cols_v, table, b, *refs):
+    refs = list(refs)[afters:]
+    outs = [[refs.pop(0) for _ in cut] for cut in cuts]
+    (sems,) = refs
     wide = ra * bs
     kw = b.shape[0]
     odd = parity[0] == 1
 
+    waits = []
     for flip in range(2):
         base = (parity[0] ^ flip) * half
         for out, (start, stop) in zip(outs[flip], cuts[flip]):
-
-            def one_row(i, _, out=out, start=start, base=base):
+            sem = sems.at[len(waits)]
+
+            def one_row(i, _, out=out, start=start, base=base, sem=sem):
                 for m in range(ra):
-                    t = cols_s[m, base + i]
                     at = pl.multiple_of(((i - start) * ra + m) * bs, bs)
-                    out[pl.ds(at, bs), :] = b[t]
+                    source = b.at[cols_s[m, base + i]]
+                    pltpu.make_async_copy(source, out.at[pl.ds(at, bs)], sem).start()
                 return 0
 
             lax.fori_loop(start, stop, one_row, 0, unroll=2)
-
-    if first:
-        scale, column = bscale[...], bcols[...]
-        rows = three_parts(scale) + [(column >> 8).astype(F32), (column & 255).astype(F32)]
-        rows.append(jnp.zeros((table.shape[0] - PARTS * rb, kw), F32))
-        table[...] = jnp.concatenate(rows, axis=0).astype(BF16)
+            blocks = out.at[pl.ds(0, (stop - start) * wide)]
+            waits.append(pltpu.make_async_copy(blocks, blocks, sem))
 
     cols = cols_v[...]
     both = [entries(cols, h * half, half, rb) for h in range(2)]
@@ -97,71 +138,41 @@
         tile = stacked(parts, META).astype(BF16)
         for out, (start, stop) in zip(outs[flip], cuts[flip]):
             out[pl.ds((stop - start) * wide, META), :] = tile
-
-    if pieces:
-        scale = ascale[...]
-        both = [entries(scale, h * half, half, rb) for h in range(2)]
-        for flip, out in enumerate(halves_of_a):
-            base = (parity[0] ^ flip) * half
-            out[pl.ds(0, half * bs), :] = a[pl.ds(pl.multiple_of(base * bs, bs), half * bs), :]
-            parts = three_parts(jnp.where(odd != (flip == 1), both[1], both[0]))
-            out[pl.ds(half * bs, META), :] = stacked(parts, META).astype(BF16)
-
-    if first:
-        tiles = acc.shape[1]
-        for i in range(acc.shape[0]):
-
-            def clear(tile, _, i=i):
-                acc[i, tile] = jnp.zeros(acc.shape[2:], F32)
-                return 0
-
-            lax.fori_loop(0, tiles, clear, 0, unroll=8)
-
-
-def gather(parity, cols, b, half, cuts, tables=None, table=None, a=None):
+    for wait in waits:
+        wait.wait()
+
+
+def gather(parity, cols, table, b, half, cuts, after):
     ra = cols.shape[0]
-    kw, bs, width = b.shape
+    bs, width = b.shape[1:]
     rb = width // bs
-    first = table is None
     smem, vmem = pl.BlockSpec(memory_space=pltpu.SMEM), pl.BlockSpec(memory_space=pltpu.VMEM)
-    args = [parity, cols, cols, in_vmem(b)]
-    specs = [smem, smem, vmem, vmem]
-    outs = [pltpu.VMEM(b.shape, BF16)]
-    if first:
-        args += tables
-        tiles = JW * bs // LANES
-        outs.append(pltpu.VMEM((32, kw), BF16))
-        outs.append(pltpu.VMEM((half, tiles, bs, LANES), F32))
-    else:
-        args.append(in_vmem(table))
-    if a is not None:
-        args += a
-        outs += [pltpu.VMEM((half * bs + META, ra * bs), BF16)] * 2
-    for cut in cuts:
-        for start, stop in cut:
-            outs.append(pltpu.VMEM(((stop - start) * ra * bs + META, width), BF16))
-    specs += [vmem] * (len(args) - len(specs))
+    hbm = pl.BlockSpec(memory_space=pltpu.HBM)
+    outs = [
+        pltpu.VMEM(((stop - start) * ra * bs + META, width), BF16) for cut in cuts for start, stop in cut
+    ]
     got = pl.pallas_call(
-        functools.partial(gather_kernel, half, ra, rb, bs, first, a is not None, cuts),
+        functools.partial(gather_kernel, half, ra, rb, bs, cuts, len(after)),
         out_shape=outs,
-        in_specs=specs,
+        in_specs=[smem, smem, vmem, vmem, hbm] + [pl.BlockSpec(memory_space=pl.ANY)] * len(after),
         out_specs=[vmem] * len(outs),
-        input_output_aliases={3: 0},
+        scratch_shapes=[pltpu.SemaphoreType.DMA((len(outs),))],
         compiler_params=pltpu.CompilerParams(vmem_limit_bytes=VMEM_LIMIT),
-        cost_estimate=pl.CostEstimate(flops=0, bytes_accessed=4 * 2**20, transcendentals=0),
+        cost_estimate=pl.CostEstimate(flops=0, bytes_accessed=1024, transcendentals=0),
         name="gather_rows",
-    )(*args)
+    )(parity, cols, cols, in_vmem(table), pltpu.with_memory_space_constraint(b, pltpu.HBM), *after)
     got = list(got)
-    messages = [[got.pop() for _ in cut][::-1] for cut in cuts[::-1]][::-1]
-    return got, messages
-
-
-def add_kernel(ra, rb, bs, flip, rows, flush, has_out, *refs):
+    return [[got.pop(0) for _ in cut] for cut in cuts]
+
+
+def add_kernel(ra, rb, bs, flip, rows, flush, has_out, place, *refs):
     refs = list(refs)
     a, b, _ = refs.pop(0), refs.pop(0), refs.pop(0)
+    a = a.at[place[0]]
     if has_out:
         refs.pop(0)
-    acc = refs.pop(0)
+    acc, done = refs.pop(0), refs.pop(0)
+    done[...] = jnp.zeros(done.shape, done.dtype)
     if flush:
         target = refs.pop(0)
     prod, scl_v, col_v, scl_s, col_s, stage, sems, out_sems = refs
@@ -223,17 +234,18 @@
             send(i).wait()
 
 
-def add_products(a, b, flip, shape, rows, acc, flush=False, out=None):
+def add_products(place, a, b, flip, shape, rows, acc, flush=False, out=None):
     half, ra, rb, bs = shape
-    out_shapes = [pltpu.VMEM(acc.shape, F32)]
+    out_shapes = [pltpu.VMEM(acc.shape, F32), jax.ShapeDtypeStruct((8, LANES), F32)]
     if flush:
         out_shapes.append(jax.ShapeDtypeStruct((half, bs, JW * bs), BF16))
     vmem = pl.BlockSpec(memory_space=pltpu.VMEM)
     anywhere = pl.BlockSpec(memory_space=pl.ANY)
-    args, specs = [a, b, in_vmem(acc)], [vmem] * 3
-    aliases = {2: 0}
+    args = [place, a, b, in_vmem(acc)]
+    specs = [pl.BlockSpec(memory_space=pltpu.SMEM)] + [vmem] * 3
+    aliases = {3: 0}
     if out is not None:
-        aliases[len(args)] = 1
+        aliases[len(args)] = 2
         args.append(out)
         specs.append(anywhere)
     count = rows[1] - rows[0]
@@ -241,7 +253,7 @@
         functools.partial(add_kernel, ra, rb, bs, flip, rows, flush, out is not None),
         out_shape=out_shapes,
         in_specs=specs,
-        out_specs=[vmem, anywhere][: len(out_shapes)],
+        out_specs=[vmem, vmem, anywhere][: len(out_shapes)],
         input_output_aliases=aliases,
         scratch_shapes=[
             pltpu.VMEM((count * ra * bs, rb * bs), F32),
@@ -254,7 +266,7 @@
             pltpu.SemaphoreType.DMA((2,)),
         ],
         compiler_params=pltpu.CompilerParams(vmem_limit_bytes=VMEM_LIMIT),
-        cost_estimate=pl.CostEstimate(flops=0, bytes_accessed=6 * 2**20, transcendentals=0),
+        cost_estimate=pl.CostEstimate(flops=0, bytes_accessed=1024, transcendentals=0),
         name="add_products",
     )(*args)
 
@@ -289,36 +301,41 @@
 
     order = sorted(range(1, panels), key=lambda by: -min(by, panels - by))
     asked = {by: named_by(by) for by in order}
+    asked[0] = a_pos
     every = (0, half)
     early = (0, half - max(1, half // 4))
     late = (early[1], half)
 
-    messages = {}
-    (b_here, table, acc), messages[0] = gather(
-        parity, a_pos, b_part, half, [[every], [every]], tables=[b_scl, b_pos]
-    )
-    for place, by in enumerate(order):
-        a = [a_part.reshape(nrows * bs, ra * bs), a_scl] if place == min(1, len(order) - 1) else None
+    table, acc = prepare(b_scl, b_pos, half, bs)
+
+    def messages(by, after):
         cuts = [[every], [early, late] if by == order[-1] else [every]]
-        got, messages[by] = gather(parity, asked[by], b_here, half, cuts, table=table, a=a)
-        b_here = got[0]
-        if a is not None:
-            kept, given = got[1:]
-    left = {0: jnp.stack([kept, step(given, 0, 1)])}
+        return gather(parity, asked[by], table, b_part, half, cuts, after)
+
+    sent = {}
+    after = [asked[by] for by in order[1:]]
+    for by in order[:-1] + [0]:
+        sent[by] = messages(by, after)
+        after = [sent[by][0][0]]
+    first = sent[order[0]][0][0]
+    kept, given = split(parity, a_part.reshape(nrows * bs, ra * bs), a_scl, half, rb, bs, first)
+    left = jnp.stack([kept, step(given, 0, 1)])
+    lefts = lax.all_gather(left, "row")
+    row = lax.axis_index("row")
+    taken = step(sent[0][1][0], 0, 1)
+    zero = jnp.zeros((1,), I32)
+    acc = add_products(zero, kept[None, None], sent[0][0][0], 0, shape, every, acc)[0]
+    acc, done = add_products(zero, left[None], taken, 1, shape, every, acc)
+    sent[order[-1]] = messages(order[-1], [done])
     for by in order:
-        pairs = [(r, (r + by) % panels) for r in range(panels)]
-        left[by] = lax.ppermute(left[0], "row", pairs)
-
-    (acc,) = add_products(kept[None], messages[0][0][0], 0, shape, every, acc)
-    (acc,) = add_products(left[0], step(messages[0][1][0], 0, 1), 1, shape, every, acc)
-    for by in order:
+        place = ((row - by) % panels).astype(I32).reshape(1)
         for flip in range(halves):
-            arrived = [step(message, by, flip) for message in messages[by][flip]]
+            arrived = [step(message, by, flip) for message in sent[by][flip]]
             if len(arrived) == 1:
-                (acc,) = add_products(left[by], arrived[0], flip, shape, every, acc)
+                acc = add_products(place, lefts, arrived[0], flip, shape, every, acc)[0]
             else:
-                acc, out = add_products(left[by], arrived[0], flip, shape, early, acc, flush=True)
-                _, out = add_products(left[by], arrived[1], flip, shape, late, acc, flush=True, out=out)
+                acc, _, out = add_products(place, lefts, arrived[0], flip, shape, early, acc, flush=True)
+                out = add_products(place, lefts, arrived[1], flip, shape, late, acc, flush=True, out=out)[2]
     return out[None, None]
 
 

time: 95.6 us -> 95.3 us (level)
  blocking collectives: 0 us -> 10.8 us
  starting transfers between devices: 22.5 us -> 15.4 us
  Pallas kernels: 29.1 us -> 35.7 us
  waiting for transfers between devices: 25.3 us -> 19.5 us
  local copies, waits for them, and re-layouts: 18.4 us -> 13 us
    all_gather x0 -> x1, blocking collectives: none -> 10.8 us  [on_device(): lefts = lax.all_gather(left, 'row')]
    ppermute x3, waiting for transfers between devices: 8.12 us -> 0.95 us  [named_by(): return lax.ppermute(a_pos, ('row', 'col'), pairs)]
    unnamed x17 -> x14, local copies, waits for them, and re-layouts: 18.4 us -> 13 us
    pallas_call x9, Pallas kernels: 22.7 us -> 27.4 us  [add_products(): pl.pallas_call(functools.partial(add_kernel, ra, rb, bs, flip, rows, flus...]
    ppermute x9, starting transfers between devices: 12.1 us -> 7.52 us  [step(): return lax.ppermute(value, 'col', pairs)]
    ppermute x3 -> x0, starting transfers between devices: 2.66 us -> none  [on_device(): left[by] = lax.ppermute(left[0], 'row', pairs)]
    pallas_call x4 -> x6, Pallas kernels: 6.35 us -> 8.32 us  [the longest x4 6.92 us: gather(): pl.pallas_call(functools.partial(gather_kernel, half, ra, rb, bs, cuts, l...]
    ppermute x9, waiting for transfers between devices: 17.1 us -> 18.6 us  [step(): return lax.ppermute(value, 'col', pairs)]
  transfers between devices with their start and end apart: 15 -> 12, of which waited for: 3 -> 3; matrix products, arithmetic and copies ran while one was open for 0% -> 0% of each run, Pallas kernels for 27% -> 29%
where the time goes in v1:
time: 95.3 us; the launch traced here: 94.7 us
  Pallas kernels  35.7 us (37%)
  waiting for transfers between devices  19.5 us (20%)
  starting transfers between devices  15.4 us (16%)
  local copies, waits for them, and re-layouts  13 us (14%)
  blocking collectives  10.8 us (11%)
    pallas_call x9, Pallas kernels, add_products(): pl.pallas_call(functools.partial(add_kernel, ra, rb, bs, flip, rows, flus...  27.4 us
    ppermute x9, waiting for transfers between devices, step(): return lax.ppermute(value, 'col', pairs)  18.6 us
    unnamed x14, local copies, waits for them, and re-layouts  13 us
    all_gather x1, blocking collectives, on_device(): lefts = lax.all_gather(left, 'row')  10.8 us
    ppermute x3, starting transfers between devices, named_by(): return lax.ppermute(a_pos, ('row', 'col'), pairs)  7.92 us
    ppermute x9, starting transfers between devices, step(): return lax.ppermute(value, 'col', pairs)  7.52 us
    pallas_call x4, Pallas kernels, gather(): pl.pallas_call(functools.partial(gather_kernel, half, ra, rb, bs, cuts, l...  6.92 us
  transfers between devices with their start and end apart: 12, of which 3 were waited for; matrix products, arithmetic and copies ran while one was open for 0% of the time, Pallas kernels for 29%

profile of v1, /device:TPU:0, one launch (start us, length us, event | category | flops | bytes accessed | tf_op | source)
XLA Modules:
  0.0 94.7 jit_solution(3494975981988639692)
XLA Ops:
  0.0 0.0 copy-start.2
  0.0 4.9 %collective-permute-start.2 = (s32[4,16]{1,0:T(4,128)}, s32[4,16]{1,0:T(4,128)S(1)}, u32[]{:S(2)}, u32[]{:S(2)}) collective-permute-start(s32[4,16]{1,0:T(4,128)} %bitcast.37), channel_id=1, source_target_pairs={{0,26},{1,27},{2,28},{3,29},{4,30},{5,31},{6,24},{7,25},{8,2},{9,3... | collective-permute-start | bytes 776 | tf_op jit(solution)/shard_map/ppermute | solution.py:300
  4.9 1.1 %collective-permute-start.1 = (s32[4,16]{1,0:T(4,128)}, s32[4,16]{1,0:T(4,128)S(1)}, u32[]{:S(2)}, u32[]{:S(2)}) collective-permute-start(s32[4,16]{1,0:T(4,128)} %bitcast.38), channel_id=1, source_target_pairs={{0,14},{1,15},{2,8},{3,9},{4,10},{5,11},{6,12},{7,13},{8,22},{9,23... | collective-permute-start | bytes 776 | tf_op jit(solution)/shard_map/ppermute | solution.py:300
  6.0 1.9 %collective-permute-start = (s32[4,16]{1,0:T(4,128)}, s32[4,16]{1,0:T(4,128)S(1)}, u32[]{:S(2)}, u32[]{:S(2)}) collective-permute-start(s32[4,16]{1,0:T(4,128)} %bitcast.39), channel_id=1, source_target_pairs={{0,20},{1,21},{2,22},{3,23},{4,16},{5,17},{6,18},{7,19},{8,28},{9,... | collective-permute-start | bytes 776 | tf_op jit(solution)/shard_map/ppermute | solution.py:300
  7.9 0.0 copy-start.3
  7.9 0.7 copy-done.3
  8.6 0.0 copy-start.4
  8.6 0.7 copy-done.4
  9.4 0.0 copy-start.5
  9.4 0.0 copy-start.6
  9.4 1.3 %prepare.1 = (bf16[32,1024]{1,0:T(8,128)(2,1)S(1)}, f32[8,128,32,128]{3,2,1,0:T(8,128)S(1)}) custom-call(f32[4,1024]{1,0:T(4,128)S(1)} %bitcast.35, s32[4,1024]{1,0:T(4,128)S(1)} %bitcast.36), custom_call_target="tpu_custom_call" | custom-call | bytes 8388608 | tf_op jit(solution)/shard_map/prepare/pallas_call | solution.py:60
  10.7 0.0 collective-permute-done.2.refs_1_.cols_s.cols_v
  10.7 0.0 collective-permute-done.1.refs_0_.cols_s.cols_v
  10.7 0.9 collective-permute-done.cols_s.cols_v
  11.6 1.7 %gather_rows.4 = (bf16[1040,128]{1,0:T(8,128)(2,1)S(1)}, bf16[1040,128]{1,0:T(8,128)(2,1)S(1)}) custom-call(s32[1]{0:T(128)} %bitcast.1.parity, s32[4,16]{1,0:T(4,128)S(1)} %collective-permute-done.cols_s.cols_v, s32[4,16]{1,0:T(4,128)S(1)} %collective-permute-done.cols_s.cols_v, bf16[32,1024]{1,0:T(8,128)(2,1)S(1)} %get-tuple-element.29.table, ...), custom_call_target="tpu_custom_call" | custom-call | bytes 1024 | tf_op jit(solution)/shard_map/gather_rows/pallas_call | solution.py:154
  13.3 1.7 %gather_rows.5 = (bf16[1040,128]{1,0:T(8,128)(2,1)S(1)}, bf16[1040,128]{1,0:T(8,128)(2,1)S(1)}) custom-call(s32[1]{0:T(128)} %bitcast.1.parity, s32[4,16]{1,0:T(4,128)S(1)} %collective-permute-done.1.refs_0_.cols_s.cols_v, s32[4,16]{1,0:T(4,128)S(1)} %collective-permute-done.1.refs_0_.cols_s.cols_v, bf16[32,1024]{1,0:T(8,128)(2,1)S(1)} %get-tuple-element.29.table, ...), custom_call_target="tpu_custom_call" | custom-call | bytes 1024 | tf_op jit(solution)/shard_map/gather_rows/pallas_call | solution.py:154
  15.0 0.0 copy-done.5
  15.0 1.7 %gather_rows.6 = (bf16[1040,128]{1,0:T(8,128)(2,1)S(1)}, bf16[1040,128]{1,0:T(8,128)(2,1)S(1)}) custom-call(s32[1]{0:T(128)} %bitcast.1.parity, s32[4,16]{1,0:T(4,128)S(1)} %bitcast.40, s32[4,16]{1,0:T(4,128)S(1)} %bitcast.41, bf16[32,1024]{1,0:T(8,128)(2,1)S(1)} %get-tuple-element.29.table, bf16[1024,32,128]{2,1,0:T(8,128)(2,1)} %bitcast.45, ...), custom_call_target="tpu_custom_call" | custom-call | bytes 1024 | tf_op jit(solution)/shard_map/gather_rows/pallas_call | solution.py:154
  16.7 0.1 collective-permute-start.4
  16.8 1.6 %collective-permute-start.10 = (bf16[1040,128]{1,0:T(8,128)(2,1)S(1)}, bf16[1040,128]{1,0:T(8,128)(2,1)S(1)}, u32[]{:S(2)}, u32[]{:S(2)}) collective-permute-start(bf16[1040,128]{1,0:T(8,128)(2,1)S(1)} %get-tuple-element.43), channel_id=1, source_target_pairs={{0,5},{1,4},{2,7},{3,6},{4,1},{5,0},{6,3},{7,2},{8,13},{9,12},{10,... | collective-permute-start | bytes 798728 | tf_op jit(solution)/shard_map/ppermute | solution.py:291
  18.4 0.0 copy-done.2
  18.4 0.0 copy-done.6
  18.4 0.1 split.1
  18.5 0.1 collective-permute-start.3
  18.7 1.4 %collective-permute-start.11 = (bf16[1040,128]{1,0:T(8,128)(2,1)S(1)}, bf16[1040,128]{1,0:T(8,128)(2,1)S(1)}, u32[]{:S(2)}, u32[]{:S(2)}) collective-permute-start(bf16[1040,128]{1,0:T(8,128)(2,1)S(1)} %get-tuple-element.30.after.refs_0_), channel_id=1, source_target_pairs={{0,4},{1,5},{2,6},{3,7},{4,0},{5,1},{6,2},{7,3},{8,12},{9,13},{10,... | collective-permute-start | bytes 798728 | tf_op jit(solution)/shard_map/ppermute | solution.py:291
  20.1 0.9 collective-permute-start.9
  21.0 2.7 %add_products.9 = (f32[8,128,32,128]{3,2,1,0:T(8,128)S(1)}, f32[8,128]{1,0:T(8,128)}) custom-call(s32[1]{0:T(128)} %constant.46.clone.1.place, bf16[1,1,272,128]{3,2,1,0:T(8,128)(2,1)S(1)} %bitcast.32, bf16[1040,128]{1,0:T(8,128)(2,1)S(1)} %get-tuple-element.35.refs_1_, ...), custom_call_target="tpu_custom_call", output_to_operand_aliasing={{0}: (3, {})} | custom-call | bytes 1024 | tf_op jit(solution)/shard_map/add_products/pallas_call | solution.py:252
  23.7 0.0 collective-permute-done.3
  23.7 0.7 collective-permute-start.8
  24.4 0.0 collective-permute-done.4.refs_1_
  24.4 2.1 %add_products.10 = (f32[8,128,32,128]{3,2,1,0:T(8,128)S(1)}, f32[8,128]{1,0:T(8,128)S(1)}) custom-call(s32[1]{0:T(128)} %constant.46.clone.1.place, bf16[1,2,272,128]{3,2,1,0:T(8,128)(2,1)S(1)} %get-tuple-element.53.refs_0_, bf16[1040,128]{1,0:T(8,128)(2,1)S(1)} %collective-permute-done.4.refs_1_, ...), custom_call_target="tpu_custom_call", output_to_operand_aliasing={{0}: (3, {})} | custom-call | bytes 1024 | tf_op jit(solution)/shard_map/add_products/pallas_call | solution.py:252
  26.6 0.0 copy-start
  26.6 5.7 %copy-done = f32[8,128,32,128]{3,2,1,0:T(8,128)} copy-done((f32[8,128,32,128]{3,2,1,0:T(8,128)}, f32[8,128,32,128]{3,2,1,0:T(8,128)S(1)}, u32[]{:S(2)}) %copy-start) | copy-done | bytes 16777240
  32.3 1.9 %gather_rows.7 = (bf16[1040,128]{1,0:T(8,128)(2,1)S(1)}, bf16[784,128]{1,0:T(8,128)(2,1)S(1)}, bf16[272,128]{1,0:T(8,128)(2,1)S(1)}) custom-call(s32[1]{0:T(128)} %bitcast.1.parity, s32[4,16]{1,0:T(4,128)S(1)} %collective-permute-done.2.refs_1_.cols_s.cols_v, s32[4,16]{1,0:T(4,128)S(1)} %collective-permute-done.2.refs_1_.cols_s.cols_v, ...), custom_call_target="tpu_custom_call" | custom-call | bytes 1024 | tf_op jit(solution)/shard_map/gather_rows/pallas_call | solution.py:154
  34.2 2.7 %collective-permute-start.7 = (bf16[1040,128]{1,0:T(8,128)(2,1)S(1)}, bf16[1040,128]{1,0:T(8,128)(2,1)S(1)}, u32[]{:S(2)}, u32[]{:S(2)}) collective-permute-start(bf16[1040,128]{1,0:T(8,128)(2,1)S(1)} %get-tuple-element.41), channel_id=1, source_target_pairs={{0,6},{1,7},{2,0},{3,1},{4,2},{5,3},{6,4},{7,5},{8,14},{9,15},{10,... | collective-permute-start | bytes 798728 | tf_op jit(solution)/shard_map/ppermute | solution.py:291
  36.9 12.2 %collective-permute-done.10.refs_1_ = bf16[1040,128]{1,0:T(8,128)(2,1)S(1)} collective-permute-done((bf16[1040,128]{1,0:T(8,128)(2,1)S(1)}, bf16[1040,128]{1,0:T(8,128)(2,1)S(1)}, u32[]{:S(2)}, u32[]{:S(2)}) %collective-permute-start.10) | collective-permute-done | bytes 266272 | tf_op jit(solution)/shard_map/ppermute | solution.py:291
  49.0 0.0 collective-permute-start.6
  49.0 6.4 %collective-permute-done.11.refs_1_ = bf16[1040,128]{1,0:T(8,128)(2,1)S(1)} collective-permute-done((bf16[1040,128]{1,0:T(8,128)(2,1)S(1)}, bf16[1040,128]{1,0:T(8,128)(2,1)S(1)}, u32[]{:S(2)}, u32[]{:S(2)}) %collective-permute-start.11) | collective-permute-done | bytes 266272 | tf_op jit(solution)/shard_map/ppermute | solution.py:291
  55.4 0.0 collective-permute-start.5
  55.4 10.8 %all-gather = bf16[8,272,128]{2,1,0:T(8,128)(2,1)S(1)} all-gather(bf16[2,272,128]{2,1,0:T(8,128)(2,1)S(1)} %get-tuple-element.54), channel_id=2, replica_groups=mesh['row'=4,'col'=8] {'row'}, dimensions={0}, use_global_device_ids=true | all-gather | bytes 696320 | tf_op jit(solution)/shard_map/all_gather | solution.py:323
  66.2 0.0 copy-start.1
  66.2 5.8 %copy-done.1 = f32[8,128,32,128]{3,2,1,0:T(8,128)S(1)} copy-done((f32[8,128,32,128]{3,2,1,0:T(8,128)S(1)}, f32[8,128,32,128]{3,2,1,0:T(8,128)}, u32[]{:S(2)}) %copy-start.1) | copy-done | bytes 16777240
  72.0 2.7 %add_products.11 = (f32[8,128,32,128]{3,2,1,0:T(8,128)S(1)}, f32[8,128]{1,0:T(8,128)}) custom-call(s32[1]{0:T(128)} %bitcast.19.place, bf16[4,2,272,128]{3,2,1,0:T(8,128)(2,1)S(1)} %bitcast.25, bf16[1040,128]{1,0:T(8,128)(2,1)S(1)} %collective-permute-done.11.refs_1_, f32[8,128,32,128]{3,2,1,0:T(8,128)S(1)} %copy-done.1), custom_call_target="tpu_custom_call", output_to_operand_aliasing={{0}: (3, {})} | custom-call | bytes 1024 | tf_op jit(solution)/shard_map/add_products/pallas_call | solution.py:252
  74.7 2.7 %add_products.12 = (f32[8,128,32,128]{3,2,1,0:T(8,128)S(1)}, f32[8,128]{1,0:T(8,128)}) custom-call(s32[1]{0:T(128)} %bitcast.19.place, bf16[4,2,272,128]{3,2,1,0:T(8,128)(2,1)S(1)} %bitcast.26, bf16[1040,128]{1,0:T(8,128)(2,1)S(1)} %collective-permute-done.10.refs_1_, f32[8,128,32,128]{3,2,1,0:T(8,128)S(1)} %get-tuple-element.45.refs_2_), custom_call_target="tpu_custom_call", output_to_operand_aliasing={{0}: (3, {})} | custom-call | bytes 1024 | tf_op jit(solution)/shard_map/add_products/pallas_call | solution.py:252
  77.4 0.0 collective-permute-done.9.refs_1_
  77.4 2.7 %add_products.13 = (f32[8,128,32,128]{3,2,1,0:T(8,128)S(1)}, f32[8,128]{1,0:T(8,128)}) custom-call(s32[1]{0:T(128)} %bitcast.18.place, bf16[4,2,272,128]{3,2,1,0:T(8,128)(2,1)S(1)} %bitcast.27, bf16[1040,128]{1,0:T(8,128)(2,1)S(1)} %collective-permute-done.9.refs_1_, f32[8,128,32,128]{3,2,1,0:T(8,128)S(1)} %get-tuple-element.46.refs_2_), custom_call_target="tpu_custom_call", output_to_operand_aliasing={{0}: (3, {})} | custom-call | bytes 1024 | tf_op jit(solution)/shard_map/add_products/pallas_call | solution.py:252
  80.1 0.0 collective-permute-done.8.refs_1_
  80.1 2.7 %add_products.14 = (f32[8,128,32,128]{3,2,1,0:T(8,128)S(1)}, f32[8,128]{1,0:T(8,128)}) custom-call(s32[1]{0:T(128)} %bitcast.18.place, bf16[4,2,272,128]{3,2,1,0:T(8,128)(2,1)S(1)} %bitcast.28, bf16[1040,128]{1,0:T(8,128)(2,1)S(1)} %collective-permute-done.8.refs_1_, f32[8,128,32,128]{3,2,1,0:T(8,128)S(1)} %get-tuple-element.47.refs_2_), custom_call_target="tpu_custom_call", output_to_operand_aliasing={{0}: (3, {})} | custom-call | bytes 1024 | tf_op jit(solution)/shard_map/add_products/pallas_call | solution.py:252
  82.9 0.0 collective-permute-done.7.refs_1_
  82.9 2.7 %add_products.15 = (f32[8,128,32,128]{3,2,1,0:T(8,128)S(1)}, f32[8,128]{1,0:T(8,128)}) custom-call(s32[1]{0:T(128)} %bitcast.place, bf16[4,2,272,128]{3,2,1,0:T(8,128)(2,1)S(1)} %bitcast.29, bf16[1040,128]{1,0:T(8,128)(2,1)S(1)} %collective-permute-done.7.refs_1_, f32[8,128,32,128]{3,2,1,0:T(8,128)S(1)} %get-tuple-element.48.refs_2_), custom_call_target="tpu_custom_call", output_to_operand_aliasing={{0}: (3, {})} | custom-call | bytes 1024 | tf_op jit(solution)/shard_map/add_products/pallas_call | solution.py:252
  85.6 0.0 collective-permute-done.6.refs_1_
  85.6 6.0 %add_products.16 = (f32[8,128,32,128]{3,2,1,0:T(8,128)S(1)}, f32[8,128]{1,0:T(8,128)}, bf16[8,32,16384]{2,1,0:T(8,128)(2,1)}) custom-call(s32[1]{0:T(128)} %bitcast.place, bf16[4,2,272,128]{3,2,1,0:T(8,128)(2,1)S(1)} %bitcast.30, bf16[784,128]{1,0:T(8,128)(2,1)S(1)} %collective-permute-done.6.refs_1_, ...), custom_call_target="tpu_custom_call", output_to_operand_aliasing={{0}: (3, {})} | custom-call | bytes 1024 | tf_op jit(solution)/shard_map/add_products/pallas_call | solution.py:252
  91.6 0.0 collective-permute-done.5.refs_1_
  91.6 3.1 %add_products.17 = (f32[8,128,32,128]{3,2,1,0:T(8,128)S(1)}, f32[8,128]{1,0:T(8,128)}, bf16[8,32,16384]{2,1,0:T(8,128)(2,1)}) custom-call(s32[1]{0:T(128)} %bitcast.place, bf16[4,2,272,128]{3,2,1,0:T(8,128)(2,1)S(1)} %bitcast.31, bf16[272,128]{1,0:T(8,128)(2,1)S(1)} %collective-permute-done.5.refs_1_, ...), custom_call_target="tpu_custom_call", output_to_operand_aliasing={{0}: (3, {}), {2}: (4, {})} | custom-call | bytes 1024 | tf_op jit(solution)/shard_map/add_products/pallas_call | solution.py:252
  (1 shorter events, 0.0 us)
Async XLA Ops:
  0.0 18.4 %copy-start.2 = (bf16[1,1,16,32,128]{4,3,2,1,0:T(8,128)(2,1)S(1)}, bf16[1,1,16,32,128]{4,3,2,1,0:T(8,128)(2,1)}, u32[]{:S(2)}) copy-start(bf16[1,1,16,32,128]{4,3,2,1,0:T(8,128)(2,1)} %param.6) | copy-start | bytes 393220
  0.0 10.7 %collective-permute-start.2 = (s32[4,16]{1,0:T(4,128)}, s32[4,16]{1,0:T(4,128)S(1)}, u32[]{:S(2)}, u32[]{:S(2)}) collective-permute-start(s32[4,16]{1,0:T(4,128)} %bitcast.37), channel_id=1, source_target_pairs={{0,26},{1,27},{2,28},{3,29},{4,30},{5,31},{6,24},{7,25},{8,2},{9,3... | collective-permute-start | bytes 776 | tf_op jit(solution)/shard_map/ppermute | solution.py:300
  4.9 5.8 %collective-permute-start.1 = (s32[4,16]{1,0:T(4,128)}, s32[4,16]{1,0:T(4,128)S(1)}, u32[]{:S(2)}, u32[]{:S(2)}) collective-permute-start(s32[4,16]{1,0:T(4,128)} %bitcast.38), channel_id=1, source_target_pairs={{0,14},{1,15},{2,8},{3,9},{4,10},{5,11},{6,12},{7,13},{8,22},{9,23... | collective-permute-start | bytes 776 | tf_op jit(solution)/shard_map/ppermute | solution.py:300
  6.0 5.6 %collective-permute-start = (s32[4,16]{1,0:T(4,128)}, s32[4,16]{1,0:T(4,128)S(1)}, u32[]{:S(2)}, u32[]{:S(2)}) collective-permute-start(s32[4,16]{1,0:T(4,128)} %bitcast.39), channel_id=1, source_target_pairs={{0,20},{1,21},{2,22},{3,23},{4,16},{5,17},{6,18},{7,19},{8,28},{9,... | collective-permute-start | bytes 776 | tf_op jit(solution)/shard_map/ppermute | solution.py:300
  7.9 0.7 copy-start.3
  8.6 0.7 copy-start.4
  9.4 5.7 %copy-start.5 = (s32[1,1,16,4]{2,3,1,0:T(4,128)S(1)}, s32[1,1,16,4]{2,3,1,0:T(4,128)}, u32[]{:S(2)}) copy-start(s32[1,1,16,4]{2,3,1,0:T(4,128)} %param.8) | copy-start | bytes 772
  9.4 9.0 %copy-start.6 = (f32[1,1,16,4]{2,3,1,0:T(4,128)S(1)}, f32[1,1,16,4]{2,3,1,0:T(4,128)}, u32[]{:S(2)}) copy-start(f32[1,1,16,4]{2,3,1,0:T(4,128)} %param.7) | copy-start | bytes 772
  16.7 7.7 %collective-permute-start.4 = (bf16[1040,128]{1,0:T(8,128)(2,1)S(1)}, bf16[1040,128]{1,0:T(8,128)(2,1)S(1)}, u32[]{:S(2)}, u32[]{:S(2)}) collective-permute-start(bf16[1040,128]{1,0:T(8,128)(2,1)S(1)} %get-tuple-element.34), channel_id=1, source_target_pairs={{0,1},{1,0},{2,3},{3,2},{4,5},{5,4},{6,7},{7,6},{8,9},{9,8},{10,11... | collective-permute-start | bytes 798728 | tf_op jit(solution)/shard_map/ppermute | solution.py:291
  16.8 32.2 %collective-permute-start.10 = (bf16[1040,128]{1,0:T(8,128)(2,1)S(1)}, bf16[1040,128]{1,0:T(8,128)(2,1)S(1)}, u32[]{:S(2)}, u32[]{:S(2)}) collective-permute-start(bf16[1040,128]{1,0:T(8,128)(2,1)S(1)} %get-tuple-element.43), channel_id=1, source_target_pairs={{0,5},{1,4},{2,7},{3,6},{4,1},{5,0},{6,3},{7,2},{8,13},{9,12},{10,... | collective-permute-start | bytes 798728 | tf_op jit(solution)/shard_map/ppermute | solution.py:291
  18.5 5.2 %collective-permute-start.3 = (bf16[272,128]{1,0:T(8,128)(2,1)S(1)}, bf16[272,128]{1,0:T(8,128)(2,1)S(1)}, u32[]{:S(2)}, u32[]{:S(2)}) collective-permute-start(bf16[272,128]{1,0:T(8,128)(2,1)S(1)} %get-tuple-element.32), channel_id=1, source_target_pairs={{0,1},{1,0},{2,3},{3,2},{4,5},{5,4},{6,7},{7,6},{8,9},{9,8},{10,11... | collective-permute-start | bytes 208904 | tf_op jit(solution)/shard_map/ppermute | solution.py:291
  18.7 36.7 %collective-permute-start.11 = (bf16[1040,128]{1,0:T(8,128)(2,1)S(1)}, bf16[1040,128]{1,0:T(8,128)(2,1)S(1)}, u32[]{:S(2)}, u32[]{:S(2)}) collective-permute-start(bf16[1040,128]{1,0:T(8,128)(2,1)S(1)} %get-tuple-element.30.after.refs_0_), channel_id=1, source_target_pairs={{0,4},{1,5},{2,6},{3,7},{4,0},{5,1},{6,2},{7,3},{8,12},{9,13},{10,... | collective-permute-start | bytes 798728 | tf_op jit(solution)/shard_map/ppermute | solution.py:291
  20.1 57.3 %collective-permute-start.9 = (bf16[1040,128]{1,0:T(8,128)(2,1)S(1)}, bf16[1040,128]{1,0:T(8,128)(2,1)S(1)}, u32[]{:S(2)}, u32[]{:S(2)}) collective-permute-start(bf16[1040,128]{1,0:T(8,128)(2,1)S(1)} %get-tuple-element.33.refs_0_), channel_id=1, source_target_pairs={{0,2},{1,3},{2,4},{3,5},{4,6},{5,7},{6,0},{7,1},{8,10},{9,11},{10,... | collective-permute-start | bytes 798728 | tf_op jit(solution)/shard_map/ppermute | solution.py:291
  23.7 56.4 %collective-permute-start.8 = (bf16[1040,128]{1,0:T(8,128)(2,1)S(1)}, bf16[1040,128]{1,0:T(8,128)(2,1)S(1)}, u32[]{:S(2)}, u32[]{:S(2)}) collective-permute-start(bf16[1040,128]{1,0:T(8,128)(2,1)S(1)} %get-tuple-element.42), channel_id=1, source_target_pairs={{0,3},{1,2},{2,5},{3,4},{4,7},{5,6},{6,1},{7,0},{8,11},{9,10},{10,... | collective-permute-start | bytes 798728 | tf_op jit(solution)/shard_map/ppermute | solution.py:291
  26.6 5.8 %copy-start = (f32[8,128,32,128]{3,2,1,0:T(8,128)}, f32[8,128,32,128]{3,2,1,0:T(8,128)S(1)}, u32[]{:S(2)}) copy-start(f32[8,128,32,128]{3,2,1,0:T(8,128)S(1)} %get-tuple-element.44.refs_2_) | copy-start | bytes 50331652
  34.2 48.7 %collective-permute-start.7 = (bf16[1040,128]{1,0:T(8,128)(2,1)S(1)}, bf16[1040,128]{1,0:T(8,128)(2,1)S(1)}, u32[]{:S(2)}, u32[]{:S(2)}) collective-permute-start(bf16[1040,128]{1,0:T(8,128)(2,1)S(1)} %get-tuple-element.41), channel_id=1, source_target_pairs={{0,6},{1,7},{2,0},{3,1},{4,2},{5,3},{6,4},{7,5},{8,14},{9,15},{10,... | collective-permute-start | bytes 798728 | tf_op jit(solution)/shard_map/ppermute | solution.py:291
  49.0 36.6 %collective-permute-start.6 = (bf16[784,128]{1,0:T(8,128)(2,1)S(1)}, bf16[784,128]{1,0:T(8,128)(2,1)S(1)}, u32[]{:S(2)}, u32[]{:S(2)}) collective-permute-start(bf16[784,128]{1,0:T(8,128)(2,1)S(1)} %get-tuple-element.40), channel_id=1, source_target_pairs={{0,7},{1,6},{2,1},{3,0},{4,3},{5,2},{6,5},{7,4},{8,15},{9,14},{10,... | collective-permute-start | bytes 602120 | tf_op jit(solution)/shard_map/ppermute | solution.py:291
  55.4 36.2 %collective-permute-start.5 = (bf16[272,128]{1,0:T(8,128)(2,1)S(1)}, bf16[272,128]{1,0:T(8,128)(2,1)S(1)}, u32[]{:S(2)}, u32[]{:S(2)}) collective-permute-start(bf16[272,128]{1,0:T(8,128)(2,1)S(1)} %get-tuple-element.39), channel_id=1, source_target_pairs={{0,7},{1,6},{2,1},{3,0},{4,3},{5,2},{6,5},{7,4},{8,15},{9,14},{10,... | collective-permute-start | bytes 208904 | tf_op jit(solution)/shard_map/ppermute | solution.py:291
  66.2 5.8 %copy-start.1 = (f32[8,128,32,128]{3,2,1,0:T(8,128)S(1)}, f32[8,128,32,128]{3,2,1,0:T(8,128)}, u32[]{:S(2)}) copy-start(f32[8,128,32,128]{3,2,1,0:T(8,128)} %copy-done) | copy-start | bytes 50331652

commit v2 on v1

--- a/solution.py
+++ b/solution.py
@@ -40,7 +40,7 @@
     return jnp.concatenate(one * rb, axis=1)
 
 
-def prepare_kernel(rb, bscale, bcols, table, acc):
+def prepare_kernel(rb, parity, bscale, bcols, table, acc):
     scale, column = bscale[...], bcols[...]
     rows = three_parts(scale) + [(column >> 8).astype(F32), (column & 255).astype(F32)]
     rows.append(jnp.zeros((table.shape[0] - PARTS * rb, table.shape[1]), F32))
@@ -54,7 +54,7 @@
         lax.fori_loop(0, acc.shape[1], clear, 0, unroll=8)
 
 
-def prepare(bscale, bcols, half, bs):
+def prepare(parity, bscale, bcols, half, bs):
     rb, kw = bscale.shape
     vmem = pl.BlockSpec(memory_space=pltpu.VMEM)
     return pl.pallas_call(
@@ -63,12 +63,12 @@
             pltpu.VMEM((-(-PARTS * rb // 16) * 16, kw), BF16),
             pltpu.VMEM((half, JW * bs // LANES, bs, LANES), F32),
         ],
-        in_specs=[vmem] * 2,
+        in_specs=[pl.BlockSpec(memory_space=pltpu.SMEM)] + [vmem] * 2,
         out_specs=[vmem] * 2,
         compiler_params=pltpu.CompilerParams(vmem_limit_bytes=VMEM_LIMIT),
-        cost_estimate=pl.CostEstimate(flops=0, bytes_accessed=8 * 2**20, transcendentals=0),
+        cost_estimate=pl.CostEstimate(flops=2 * 10**10, bytes_accessed=2**20, transcendentals=0),
         name="prepare",
-    )(bscale, bcols)
+    )(parity, bscale, bcols)
 
 
 def split_kernel(half, rb, bs, parity, a, ascale, after, kept, given):
@@ -90,9 +90,28 @@
         in_specs=[smem, vmem, vmem, pl.BlockSpec(memory_space=pl.ANY)],
         out_specs=[vmem] * 2,
         compiler_params=pltpu.CompilerParams(vmem_limit_bytes=VMEM_LIMIT),
-        cost_estimate=pl.CostEstimate(flops=0, bytes_accessed=1024, transcendentals=0),
+        cost_estimate=pl.CostEstimate(flops=2 * 10**10, bytes_accessed=2**20, transcendentals=0),
         name="split",
     )(parity, a, ascale, after)
+
+
+def join_kernel(own, taken, both):
+    count = own.shape[0]
+    both[pl.ds(0, count)] = own[...]
+    both[pl.ds(count, count)] = taken[...]
+
+
+def join(own, taken):
+    vmem = pl.BlockSpec(memory_space=pltpu.VMEM)
+    return pl.pallas_call(
+        join_kernel,
+        out_shape=pltpu.VMEM((2 * own.shape[0],) + own.shape[1:], BF16),
+        in_specs=[vmem] * 2,
+        out_specs=vmem,
+        compiler_params=pltpu.CompilerParams(vmem_limit_bytes=VMEM_LIMIT),
+        cost_estimate=pl.CostEstimate(flops=2 * 10**10, bytes_accessed=2**20, transcendentals=0),
+        name="join",
+    )(in_vmem(own), taken)
 
 
 def gather_kernel(half, ra, rb, bs, cuts, afters, parity, cols_s, cols_v, table, b, *refs):
@@ -122,7 +141,7 @@
 
     cols = cols_v[...]
     both = [entries(cols, h * half, half, rb) for h in range(2)]
-    for flip in range(2):
+    for flip in [flip for flip in range(2) if cuts[flip]]:
         named = jnp.where(odd != (flip == 1), both[1], both[0])
         named = jnp.broadcast_to(named, (kw, named.shape[1]))
         picked = lax.broadcasted_iota(I32, named.shape, 0) == named
@@ -158,17 +177,18 @@
         out_specs=[vmem] * len(outs),
         scratch_shapes=[pltpu.SemaphoreType.DMA((len(outs),))],
         compiler_params=pltpu.CompilerParams(vmem_limit_bytes=VMEM_LIMIT),
-        cost_estimate=pl.CostEstimate(flops=0, bytes_accessed=1024, transcendentals=0),
+        cost_estimate=pl.CostEstimate(flops=2 * 10**10, bytes_accessed=2**20, transcendentals=0),
         name="gather_rows",
     )(parity, cols, cols, in_vmem(table), pltpu.with_memory_space_constraint(b, pltpu.HBM), *after)
     got = list(got)
     return [[got.pop(0) for _ in cut] for cut in cuts]
 
 
-def add_kernel(ra, rb, bs, flip, rows, flush, has_out, place, *refs):
+def add_kernel(ra, rb, bs, by, flip, rows, flush, afters, has_out, info, *refs):
     refs = list(refs)
     a, b, _ = refs.pop(0), refs.pop(0), refs.pop(0)
-    a = a.at[place[0]]
+    refs = refs[afters:]
+    a = a.at[info[1 + by]]
     if has_out:
         refs.pop(0)
     acc, done = refs.pop(0), refs.pop(0)
@@ -234,23 +254,25 @@
             send(i).wait()
 
 
-def add_products(place, a, b, flip, shape, rows, acc, flush=False, out=None):
+def add_products(info, a, b, by, flip, shape, rows, acc, flush=False, out=None, after=()):
     half, ra, rb, bs = shape
     out_shapes = [pltpu.VMEM(acc.shape, F32), jax.ShapeDtypeStruct((8, LANES), F32)]
     if flush:
         out_shapes.append(jax.ShapeDtypeStruct((half, bs, JW * bs), BF16))
     vmem = pl.BlockSpec(memory_space=pltpu.VMEM)
     anywhere = pl.BlockSpec(memory_space=pl.ANY)
-    args = [place, a, b, in_vmem(acc)]
+    args = [info, in_vmem(a), b, in_vmem(acc)]
     specs = [pl.BlockSpec(memory_space=pltpu.SMEM)] + [vmem] * 3
     aliases = {3: 0}
+    args += after
+    specs += [anywhere] * len(after)
     if out is not None:
         aliases[len(args)] = 2
         args.append(out)
         specs.append(anywhere)
     count = rows[1] - rows[0]
     return pl.pallas_call(
-        functools.partial(add_kernel, ra, rb, bs, flip, rows, flush, out is not None),
+        functools.partial(add_kernel, ra, rb, bs, by, flip, rows, flush, len(after), out is not None),
         out_shape=out_shapes,
         in_specs=specs,
         out_specs=[vmem, vmem, anywhere][: len(out_shapes)],
@@ -266,7 +288,7 @@
             pltpu.SemaphoreType.DMA((2,)),
         ],
         compiler_params=pltpu.CompilerParams(vmem_limit_bytes=VMEM_LIMIT),
-        cost_estimate=pl.CostEstimate(flops=0, bytes_accessed=1024, transcendentals=0),
+        cost_estimate=pl.CostEstimate(flops=2 * 10**10, bytes_accessed=2**20, transcendentals=0),
         name="add_products",
     )(*args)
 
@@ -282,7 +304,9 @@
     ra, rb = a_scl.shape[0], b_scl.shape[0]
     half = nrows // halves
     shape = (half, ra, rb, bs)
-    parity = (lax.axis_index("col") % halves).astype(I32).reshape(1)
+    row = lax.axis_index("row")
+    parity = lax.axis_index("col") % halves
+    info = jnp.stack([parity] + [row ^ ((row - by) % panels) for by in range(panels)]).astype(I32)
 
     def step(value, by, flip):
         pairs = [
@@ -306,36 +330,45 @@
     early = (0, half - max(1, half // 4))
     late = (early[1], half)
 
-    table, acc = prepare(b_scl, b_pos, half, bs)
-
-    def messages(by, after):
-        cuts = [[every], [early, late] if by == order[-1] else [every]]
-        return gather(parity, asked[by], table, b_part, half, cuts, after)
-
-    sent = {}
-    after = [asked[by] for by in order[1:]]
-    for by in order[:-1] + [0]:
-        sent[by] = messages(by, after)
+    table, acc = prepare(info, b_scl, b_pos, half, bs)
+
+    def messages(by, cuts, after):
+        return gather(info, asked[by], table, b_part, half, cuts, after)
+
+    whole = [[every], [every]]
+    sent = {order[0]: messages(order[0], whole, [asked[by] for by in order[1:]])}
+    first = sent[order[0]][0][0]
+    kept, given = split(info, a_part.reshape(nrows * bs, ra * bs), a_scl, half, rb, bs, first)
+    left = join(kept[None], step(given, 0, 1)[None])[None]
+    own_left = left
+    bit = 1
+    while bit < panels:
+        left = join(left, lax.ppermute(left, "row", [(r, r ^ bit) for r in range(panels)]))
+        bit *= 2
+    after = [first]
+    for by in order[1:-1] + [0]:
+        sent[by] = messages(by, whole, after)
         after = [sent[by][0][0]]
-    first = sent[order[0]][0][0]
-    kept, given = split(parity, a_part.reshape(nrows * bs, ra * bs), a_scl, half, rb, bs, first)
-    left = jnp.stack([kept, step(given, 0, 1)])
-    lefts = lax.all_gather(left, "row")
-    row = lax.axis_index("row")
     taken = step(sent[0][1][0], 0, 1)
-    zero = jnp.zeros((1,), I32)
-    acc = add_products(zero, kept[None, None], sent[0][0][0], 0, shape, every, acc)[0]
-    acc, done = add_products(zero, left[None], taken, 1, shape, every, acc)
-    sent[order[-1]] = messages(order[-1], [done])
-    for by in order:
-        place = ((row - by) % panels).astype(I32).reshape(1)
+    acc, done = add_products(info, own_left, sent[0][0][0], 0, 0, shape, every, acc)
+    last = order[-1]
+    ends = [messages(last, [[every], []], [done, left])[0][0]]
+    for by in order[:-1]:
         for flip in range(halves):
-            arrived = [step(message, by, flip) for message in sent[by][flip]]
-            if len(arrived) == 1:
-                acc = add_products(place, lefts, arrived[0], flip, shape, every, acc)[0]
-            else:
-                acc, _, out = add_products(place, lefts, arrived[0], flip, shape, early, acc, flush=True)
-                out = add_products(place, lefts, arrived[1], flip, shape, late, acc, flush=True, out=out)[2]
+            arrived = step(sent[by][flip][0], by, flip)
+            after = ends[-1:] if by == order[0] else []
+            acc, done = add_products(info, left, arrived, by, flip, shape, every, acc, after=after)
+            if by == order[0]:
+                rows = early if flip == 0 else late
+                ends.append(messages(last, [[], [rows]], [done])[1][0])
+        if by == order[0]:
+            acc = add_products(info, left, taken, 0, 1, shape, every, acc)[0]
+    arrived = step(ends[0], last, 0)
+    acc = add_products(info, left, arrived, last, 0, shape, every, acc)[0]
+    arrived = step(ends[1], last, 1)
+    acc, _, out = add_products(info, left, arrived, last, 1, shape, early, acc, flush=True)
+    arrived = step(ends[2], last, 1)
+    out = add_products(info, left, arrived, last, 1, shape, late, acc, flush=True, out=out)[2]
     return out[None, None]
 
 

time: 95.3 us -> 81.7 us (0.86)
  local copies, waits for them, and re-layouts: 13 us -> 1.53 us
  blocking collectives: 10.8 us -> 0 us
  Pallas kernels: 35.7 us -> 46 us
  waiting for transfers between devices: 19.5 us -> 14.1 us
  starting transfers between devices: 15.4 us -> 19.1 us
    unnamed x14 -> x10, local copies, waits for them, and re-layouts: 13 us -> 1.45 us
    all_gather x1 -> x0, blocking collectives: 10.8 us -> none  [on_device(): lefts = lax.all_gather(left, 'row')]
    ppermute x9, waiting for transfers between devices: 18.6 us -> 8.57 us  [step(): return lax.ppermute(value, 'col', pairs)]
    ppermute x0 -> x2, waiting for transfers between devices: none -> 5.23 us  [on_device(): lax.ppermute(left, 'row', [(r, r ^ bit) for r in range(panels)])]
    pallas_call x9 -> x12, Pallas kernels: 27.4 us -> 32.4 us  [the longest x9 32.3 us: add_products(): pl.pallas_call(functools.partial(add_kernel, ra, rb, bs, by, flip, rows,...]
    pallas_call x4 -> x6, Pallas kernels: 6.92 us -> 11.2 us  [gather(): pl.pallas_call(functools.partial(gather_kernel, half, ra, rb, bs, cuts, l...]
    ppermute x0 -> x2, starting transfers between devices: none -> 2.15 us  [on_device(): lax.ppermute(left, 'row', [(r, r ^ bit) for r in range(panels)])]
    ppermute x9, starting transfers between devices: 7.52 us -> 9.04 us  [step(): return lax.ppermute(value, 'col', pairs)]
  transfers between devices with their start and end apart: 12 -> 14, of which waited for: 3 -> 3; matrix products, arithmetic and copies ran while one was open for 0% -> 0% of each run, Pallas kernels for 29% -> 49%
where the time goes in v2:
time: 81.7 us; the launch traced here: 81 us
  Pallas kernels  46 us (56%)
  starting transfers between devices  19.1 us (23%)
  waiting for transfers between devices  14.1 us (17%)
  local copies, waits for them, and re-layouts  1.53 us (2%)
    pallas_call x9, Pallas kernels, add_products(): pl.pallas_call(functools.partial(add_kernel, ra, rb, bs, by, flip, rows,...  32.3 us
    pallas_call x6, Pallas kernels, gather(): pl.pallas_call(functools.partial(gather_kernel, half, ra, rb, bs, cuts, l...  11.2 us
    ppermute x9, starting transfers between devices, step(): return lax.ppermute(value, 'col', pairs)  9.04 us
    ppermute x9, waiting for transfers between devices, step(): return lax.ppermute(value, 'col', pairs)  8.57 us
    ppermute x3, starting transfers between devices, named_by(): return lax.ppermute(a_pos, ('row', 'col'), pairs)  7.92 us
    ppermute x2, waiting for transfers between devices, on_device(): lax.ppermute(left, 'row', [(r, r ^ bit) for r in range(panels)])  5.23 us
    ppermute x2, starting transfers between devices, on_device(): lax.ppermute(left, 'row', [(r, r ^ bit) for r in range(panels)])  2.15 us
    pallas_call x1, Pallas kernels, prepare(): pl.pallas_call(functools.partial(prepare_kernel, rb), out_shape=[pltpu.VM...  1.83 us
  transfers between devices with their start and end apart: 14, of which 3 were waited for; matrix products, arithmetic and copies ran while one was open for 0% of the time, Pallas kernels for 49%

profile of v2, /device:TPU:0, one launch (start us, length us, event | category | flops | bytes accessed | tf_op | source)
XLA Modules:
  0.0 81.0 jit_solution(10303955080382806934)
XLA Ops:
  0.0 4.9 %collective-permute-start.2 = (s32[4,16]{1,0:T(4,128)}, s32[4,16]{1,0:T(4,128)S(1)}, u32[]{:S(2)}, u32[]{:S(2)}) collective-permute-start(s32[4,16]{1,0:T(4,128)} %bitcast.31), channel_id=1, source_target_pairs={{0,26},{1,27},{2,28},{3,29},{4,30},{5,31},{6,24},{7,25},{8,2},{9,3... | collective-permute-start | bytes 776 | tf_op jit(solution)/shard_map/ppermute | solution.py:324
  4.9 1.1 %collective-permute-start.1 = (s32[4,16]{1,0:T(4,128)}, s32[4,16]{1,0:T(4,128)S(1)}, u32[]{:S(2)}, u32[]{:S(2)}) collective-permute-start(s32[4,16]{1,0:T(4,128)} %bitcast.32), channel_id=1, source_target_pairs={{0,14},{1,15},{2,8},{3,9},{4,10},{5,11},{6,12},{7,13},{8,22},{9,23... | collective-permute-start | bytes 776 | tf_op jit(solution)/shard_map/ppermute | solution.py:324
  6.0 1.9 %collective-permute-start = (s32[4,16]{1,0:T(4,128)}, s32[4,16]{1,0:T(4,128)S(1)}, u32[]{:S(2)}, u32[]{:S(2)}) collective-permute-start(s32[4,16]{1,0:T(4,128)} %bitcast.33), channel_id=1, source_target_pairs={{0,20},{1,21},{2,22},{3,23},{4,16},{5,17},{6,18},{7,19},{8,28},{9,... | collective-permute-start | bytes 776 | tf_op jit(solution)/shard_map/ppermute | solution.py:324
  7.9 0.1 stack.23.parity.info
  8.0 0.0 copy-start.1
  8.0 0.7 copy-done.1
  8.7 0.0 copy-start.2
  8.7 0.7 copy-done.2
  9.4 1.8 %prepare.1 = (bf16[32,1024]{1,0:T(8,128)(2,1)S(1)}, f32[8,128,32,128]{3,2,1,0:T(8,128)S(1)}) custom-call(s32[5]{0:T(128)S(1)} %stack.23.parity.info, f32[4,1024]{1,0:T(4,128)S(1)} %bitcast.28, s32[4,1024]{1,0:T(4,128)S(1)} %bitcast.29), custom_call_target="tpu_custom_call" | custom-call | flops 20000000000 | bytes 1048576 | tf_op jit(solution)/shard_map/prepare/pallas_call | solution.py:60
  11.3 0.0 collective-permute-done.2.refs_1_.cols_s.cols_v
  11.3 0.0 collective-permute-done.1.refs_0_.cols_s.cols_v
  11.3 0.3 collective-permute-done.cols_s.cols_v
  11.6 0.0 copy-start
  11.6 0.0 copy-start.3
  11.6 2.4 %gather_rows.6 = (bf16[1040,128]{1,0:T(8,128)(2,1)}, bf16[1040,128]{1,0:T(8,128)(2,1)S(1)}) custom-call(s32[5]{0:T(128)S(1)} %stack.23.parity.info, s32[4,16]{1,0:T(4,128)S(1)} %collective-permute-done.cols_s.cols_v, s32[4,16]{1,0:T(4,128)S(1)} %collective-permute-done.cols_s.cols_v, bf16[32,1024]{1,0:T(8,128)(2,1)S(1)} %get-tuple-element.28.table, ...), custom_call_target="tpu_custom_call" | custom-call | flops 20000000000 | bytes 1048576 | tf_op jit(solution)/shard_map/gather_rows/pallas_call | solution.py:173
  14.0 2.0 %collective-permute-start.7 = (bf16[1040,128]{1,0:T(8,128)(2,1)}, bf16[1040,128]{1,0:T(8,128)(2,1)}, u32[]{:S(2)}, u32[]{:S(2)}) collective-permute-start(bf16[1040,128]{1,0:T(8,128)(2,1)} %get-tuple-element.29.after.refs_0_), channel_id=1, source_target_pairs={{0,4},{1,5},{2,6},{3,7},{4,0},{5,1},{6,2},{7,3},{8,12},{9,13},{10,... | collective-permute-start | bytes 798728 | tf_op jit(solution)/shard_map/ppermute | solution.py:315
  15.9 0.0 copy-done
  15.9 0.0 copy-done.3
  15.9 0.6 split.1
  16.6 0.1 collective-permute-start.3
  16.7 2.5 %gather_rows.7 = (bf16[1040,128]{1,0:T(8,128)(2,1)}, bf16[1040,128]{1,0:T(8,128)(2,1)}) custom-call(s32[5]{0:T(128)S(1)} %stack.23.parity.info, s32[4,16]{1,0:T(4,128)S(1)} %collective-permute-done.1.refs_0_.cols_s.cols_v, s32[4,16]{1,0:T(4,128)S(1)} %collective-permute-done.1.refs_0_.cols_s.cols_v, bf16[32,1024]{1,0:T(8,128)(2,1)S(1)} %get-tuple-element.28.table, ...), custom_call_target="tpu_custom_call" | custom-call | flops 20000000000 | bytes 1048576 | tf_op jit(solution)/shard_map/gather_rows/pallas_call | solution.py:173
  19.2 1.7 %collective-permute-start.12 = (bf16[1040,128]{1,0:T(8,128)(2,1)}, bf16[1040,128]{1,0:T(8,128)(2,1)}, u32[]{:S(2)}, u32[]{:S(2)}) collective-permute-start(bf16[1040,128]{1,0:T(8,128)(2,1)} %get-tuple-element.33.refs_0_), channel_id=1, source_target_pairs={{0,2},{1,3},{2,4},{3,5},{4,6},{5,7},{6,0},{7,1},{8,10},{9,11},{10,... | collective-permute-start | bytes 798728 | tf_op jit(solution)/shard_map/ppermute | solution.py:315
  20.9 0.0 collective-permute-done.3
  20.9 0.0 copy-start.4
  20.9 1.5 %collective-permute-start.4 = (bf16[1,2,272,128]{3,2,1,0:T(8,128)(2,1)S(1)}, bf16[1,2,272,128]{3,2,1,0:T(8,128)(2,1)S(1)}, u32[]{:S(2)}, u32[]{:S(2)}) collective-permute-start(bf16[1,2,272,128]{3,2,1,0:T(8,128)(2,1)S(1)} %bitcast.23), channel_id=1, source_target_pairs={{0,8},{8,0},{16,24},{24,16},{1,9},{9,1},{17,25},{25,17},{2,10},{10... | collective-permute-start | bytes 417800 | tf_op jit(solution)/shard_map/ppermute | solution.py:346
  22.4 0.0 copy-done.4
  22.4 1.7 %gather_rows.8 = (bf16[1040,128]{1,0:T(8,128)(2,1)S(1)}, bf16[1040,128]{1,0:T(8,128)(2,1)S(1)}) custom-call(s32[5]{0:T(128)S(1)} %stack.23.parity.info, s32[4,16]{1,0:T(4,128)S(1)} %bitcast.34, s32[4,16]{1,0:T(4,128)S(1)} %bitcast.35, bf16[32,1024]{1,0:T(8,128)(2,1)S(1)} %get-tuple-element.28.table, bf16[1024,32,128]{2,1,0:T(8,128)(2,1)} %bitcast.39, ...), custom_call_target="tpu_custom_call" | custom-call | flops 20000000000 | bytes 1048576 | tf_op jit(solution)/shard_map/gather_rows/pallas_call | solution.py:173
  24.1 1.3 %collective-permute-start.6 = (bf16[1040,128]{1,0:T(8,128)(2,1)S(1)}, bf16[1040,128]{1,0:T(8,128)(2,1)S(1)}, u32[]{:S(2)}, u32[]{:S(2)}) collective-permute-start(bf16[1040,128]{1,0:T(8,128)(2,1)S(1)} %get-tuple-element.32), channel_id=1, source_target_pairs={{0,5},{1,4},{2,7},{3,6},{4,1},{5,0},{6,3},{7,2},{8,13},{9,12},{10,... | collective-permute-start | bytes 798728 | tf_op jit(solution)/shard_map/ppermute | solution.py:315
  25.4 2.2 %collective-permute-start.11 = (bf16[1040,128]{1,0:T(8,128)(2,1)}, bf16[1040,128]{1,0:T(8,128)(2,1)}, u32[]{:S(2)}, u32[]{:S(2)}) collective-permute-start(bf16[1040,128]{1,0:T(8,128)(2,1)} %get-tuple-element.41), channel_id=1, source_target_pairs={{0,3},{1,2},{2,5},{3,4},{4,7},{5,6},{6,1},{7,0},{8,11},{9,10},{10,... | collective-permute-start | bytes 798728 | tf_op jit(solution)/shard_map/ppermute | solution.py:315
  27.6 0.0 collective-permute-done.4.taken
  27.6 0.7 collective-permute-start.5
  28.3 2.6 %add_products.9 = (f32[8,128,32,128]{3,2,1,0:T(8,128)S(1)}, f32[8,128]{1,0:T(8,128)S(1)}) custom-call(s32[5]{0:T(128)S(1)} %stack.23.parity.info, bf16[1,2,272,128]{3,2,1,0:T(8,128)(2,1)S(1)} %bitcast.25, bf16[1040,128]{1,0:T(8,128)(2,1)S(1)} %get-tuple-element.34.refs_1_, ...), custom_call_target="tpu_custom_call", output_to_operand_aliasing={{0}: (3, {})} | custom-call | flops 20000000000 | bytes 1048576 | tf_op jit(solution)/shard_map/add_products/pallas_call | solution.py:274
  30.9 5.2 %collective-permute-done.5.taken = bf16[2,2,272,128]{3,2,1,0:T(8,128)(2,1)S(1)} collective-permute-done((bf16[2,2,272,128]{3,2,1,0:T(8,128)(2,1)S(1)}, bf16[2,2,272,128]{3,2,1,0:T(8,128)(2,1)S(1)}, u32[]{:S(2)}, u32[]{:S(2)}) %collective-permute-start.5) | collective-permute-done | bytes 278560 | tf_op jit(solution)/shard_map/ppermute | solution.py:346
  36.2 0.0 collective-permute-start.13
  36.2 1.5 %gather_rows.9.refs_3_ = bf16[1040,128]{1,0:T(8,128)(2,1)S(1)} custom-call(s32[5]{0:T(128)S(1)} %stack.23.parity.info, s32[4,16]{1,0:T(4,128)S(1)} %collective-permute-done.2.refs_1_.cols_s.cols_v, s32[4,16]{1,0:T(4,128)S(1)} %collective-permute-done.2.refs_1_.cols_s.cols_v, bf16[32,1024]{1,0:T(8,128)(2,1)S(1)} %get-tuple-element.28.table, ...), custom_call_target="tpu_custom_call" | custom-call | flops 20000000000 | bytes 1048576 | tf_op jit(solution)/shard_map/gather_rows/pallas_call | solution.py:173
  37.8 8.6 %collective-permute-done.7.refs_1_ = bf16[1040,128]{1,0:T(8,128)(2,1)} collective-permute-done((bf16[1040,128]{1,0:T(8,128)(2,1)}, bf16[1040,128]{1,0:T(8,128)(2,1)}, u32[]{:S(2)}, u32[]{:S(2)}) %collective-permute-start.7) | collective-permute-done | bytes 266272 | tf_op jit(solution)/shard_map/ppermute | solution.py:315
  46.3 0.0 collective-permute-start.10
  46.3 3.1 %add_products.10 = (f32[8,128,32,128]{3,2,1,0:T(8,128)S(1)}, f32[8,128]{1,0:T(8,128)S(1)}) custom-call(s32[5]{0:T(128)S(1)} %stack.23.parity.info, bf16[4,2,272,128]{3,2,1,0:T(8,128)(2,1)S(1)} %join.5.refs_1_.refs_0_, bf16[1040,128]{1,0:T(8,128)(2,1)} %collective-permute-done.7.refs_1_, ...), custom_call_target="tpu_custom_call", output_to_operand_aliasing={{0}: (3, {})} | custom-call | flops 20000000000 | bytes 1048576 | tf_op jit(solution)/shard_map/add_products/pallas_call | solution.py:274
  49.4 1.5 %gather_rows.10.refs_3_ = bf16[784,128]{1,0:T(8,128)(2,1)S(1)} custom-call(s32[5]{0:T(128)S(1)} %stack.23.parity.info, s32[4,16]{1,0:T(4,128)S(1)} %collective-permute-done.2.refs_1_.cols_s.cols_v, s32[4,16]{1,0:T(4,128)S(1)} %collective-permute-done.2.refs_1_.cols_s.cols_v, bf16[32,1024]{1,0:T(8,128)(2,1)S(1)} %get-tuple-element.28.table, ...), custom_call_target="tpu_custom_call" | custom-call | flops 20000000000 | bytes 1048576 | tf_op jit(solution)/shard_map/gather_rows/pallas_call | solution.py:173
  50.9 0.0 collective-permute-done.6.refs_1_
  50.9 0.1 collective-permute-start.9
  51.0 2.7 %add_products.11 = (f32[8,128,32,128]{3,2,1,0:T(8,128)S(1)}, f32[8,128]{1,0:T(8,128)S(1)}) custom-call(s32[5]{0:T(128)S(1)} %stack.23.parity.info, bf16[4,2,272,128]{3,2,1,0:T(8,128)(2,1)S(1)} %join.5.refs_1_.refs_0_, bf16[1040,128]{1,0:T(8,128)(2,1)S(1)} %collective-permute-done.6.refs_1_, ...), custom_call_target="tpu_custom_call", output_to_operand_aliasing={{0}: (3, {})} | custom-call | flops 20000000000 | bytes 1048576 | tf_op jit(solution)/shard_map/add_products/pallas_call | solution.py:274
  53.6 1.5 %gather_rows.11 = bf16[272,128]{1,0:T(8,128)(2,1)S(1)} custom-call(s32[5]{0:T(128)S(1)} %stack.23.parity.info, s32[4,16]{1,0:T(4,128)S(1)} %collective-permute-done.2.refs_1_.cols_s.cols_v, s32[4,16]{1,0:T(4,128)S(1)} %collective-permute-done.2.refs_1_.cols_s.cols_v, bf16[32,1024]{1,0:T(8,128)(2,1)S(1)} %get-tuple-element.28.table, ...), custom_call_target="tpu_custom_call" | custom-call | flops 20000000000 | bytes 1048576 | tf_op jit(solution)/shard_map/gather_rows/pallas_call | solution.py:173
  55.2 0.0 collective-permute-done.13.refs_1_
  55.2 1.7 %collective-permute-start.8 = (bf16[272,128]{1,0:T(8,128)(2,1)S(1)}, bf16[272,128]{1,0:T(8,128)(2,1)S(1)}, u32[]{:S(2)}, u32[]{:S(2)}) collective-permute-start(bf16[272,128]{1,0:T(8,128)(2,1)S(1)} %gather_rows.11), channel_id=1, source_target_pairs={{0,7},{1,6},{2,1},{3,0},{4,3},{5,2},{6,5},{7,4},{8,15},{9,14},{10,... | collective-permute-start | bytes 208904 | tf_op jit(solution)/shard_map/ppermute | solution.py:315
  56.9 3.2 %add_products.12 = (f32[8,128,32,128]{3,2,1,0:T(8,128)S(1)}, f32[8,128]{1,0:T(8,128)}) custom-call(s32[5]{0:T(128)S(1)} %stack.23.parity.info, bf16[4,2,272,128]{3,2,1,0:T(8,128)(2,1)S(1)} %join.5.refs_1_.refs_0_, bf16[1040,128]{1,0:T(8,128)(2,1)S(1)} %collective-permute-done.13.refs_1_, ...), custom_call_target="tpu_custom_call", output_to_operand_aliasing={{0}: (3, {})} | custom-call | flops 20000000000 | bytes 1048576 | tf_op jit(solution)/shard_map/add_products/pallas_call | solution.py:274
  60.2 0.0 collective-permute-done.12.refs_1_
  60.2 3.7 %add_products.13 = (f32[8,128,32,128]{3,2,1,0:T(8,128)S(1)}, f32[8,128]{1,0:T(8,128)}) custom-call(s32[5]{0:T(128)S(1)} %stack.23.parity.info, bf16[4,2,272,128]{3,2,1,0:T(8,128)(2,1)S(1)} %join.5.refs_1_.refs_0_, bf16[1040,128]{1,0:T(8,128)(2,1)} %collective-permute-done.12.refs_1_, ...), custom_call_target="tpu_custom_call", output_to_operand_aliasing={{0}: (3, {})} | custom-call | flops 20000000000 | bytes 1048576 | tf_op jit(solution)/shard_map/add_products/pallas_call | solution.py:274
  63.9 0.0 collective-permute-done.11.refs_1_
  63.9 3.7 %add_products.14 = (f32[8,128,32,128]{3,2,1,0:T(8,128)S(1)}, f32[8,128]{1,0:T(8,128)}) custom-call(s32[5]{0:T(128)S(1)} %stack.23.parity.info, bf16[4,2,272,128]{3,2,1,0:T(8,128)(2,1)S(1)} %join.5.refs_1_.refs_0_, bf16[1040,128]{1,0:T(8,128)(2,1)} %collective-permute-done.11.refs_1_, ...), custom_call_target="tpu_custom_call", output_to_operand_aliasing={{0}: (3, {})} | custom-call | flops 20000000000 | bytes 1048576 | tf_op jit(solution)/shard_map/add_products/pallas_call | solution.py:274
  67.5 0.0 collective-permute-done.10.refs_1_
  67.5 3.2 %add_products.15 = (f32[8,128,32,128]{3,2,1,0:T(8,128)S(1)}, f32[8,128]{1,0:T(8,128)}) custom-call(s32[5]{0:T(128)S(1)} %stack.23.parity.info, bf16[4,2,272,128]{3,2,1,0:T(8,128)(2,1)S(1)} %join.5.refs_1_.refs_0_, bf16[1040,128]{1,0:T(8,128)(2,1)S(1)} %collective-permute-done.10.refs_1_, ...), custom_call_target="tpu_custom_call", output_to_operand_aliasing={{0}: (3, {})} | custom-call | flops 20000000000 | bytes 1048576 | tf_op jit(solution)/shard_map/add_products/pallas_call | solution.py:274
  70.8 0.0 collective-permute-done.9.refs_1_
  70.8 6.5 %add_products.16 = (f32[8,128,32,128]{3,2,1,0:T(8,128)S(1)}, f32[8,128]{1,0:T(8,128)}, bf16[8,32,16384]{2,1,0:T(8,128)(2,1)}) custom-call(s32[5]{0:T(128)S(1)} %stack.23.parity.info, bf16[4,2,272,128]{3,2,1,0:T(8,128)(2,1)S(1)} %join.5.refs_1_.refs_0_, bf16[784,128]{1,0:T(8,128)(2,1)S(1)} %collective-permute-done.9.refs_1_, ...), custom_call_target="tpu_custom_call", output_to_operand_aliasing={{0}: (3, {})} | custom-call | flops 20000000000 | bytes 1048576 | tf_op jit(solution)/shard_map/add_products/pallas_call | solution.py:274
  77.4 0.0 collective-permute-done.8.refs_1_
  77.4 3.6 %add_products.17 = (f32[8,128,32,128]{3,2,1,0:T(8,128)S(1)}, f32[8,128]{1,0:T(8,128)}, bf16[8,32,16384]{2,1,0:T(8,128)(2,1)}) custom-call(s32[5]{0:T(128)S(1)} %stack.23.parity.info, bf16[4,2,272,128]{3,2,1,0:T(8,128)(2,1)S(1)} %join.5.refs_1_.refs_0_, ...), custom_call_target="tpu_custom_call", output_to_operand_aliasing={{0}: (3, {}), {2}: (4, {})} | custom-call | flops 20000000000 | bytes 1048576 | tf_op jit(solution)/shard_map/add_products/pallas_call | solution.py:274
  (3 shorter events, 0.1 us)
Async XLA Ops:
  0.0 11.3 %collective-permute-start.2 = (s32[4,16]{1,0:T(4,128)}, s32[4,16]{1,0:T(4,128)S(1)}, u32[]{:S(2)}, u32[]{:S(2)}) collective-permute-start(s32[4,16]{1,0:T(4,128)} %bitcast.31), channel_id=1, source_target_pairs={{0,26},{1,27},{2,28},{3,29},{4,30},{5,31},{6,24},{7,25},{8,2},{9,3... | collective-permute-start | bytes 776 | tf_op jit(solution)/shard_map/ppermute | solution.py:324
  4.9 6.4 %collective-permute-start.1 = (s32[4,16]{1,0:T(4,128)}, s32[4,16]{1,0:T(4,128)S(1)}, u32[]{:S(2)}, u32[]{:S(2)}) collective-permute-start(s32[4,16]{1,0:T(4,128)} %bitcast.32), channel_id=1, source_target_pairs={{0,14},{1,15},{2,8},{3,9},{4,10},{5,11},{6,12},{7,13},{8,22},{9,23... | collective-permute-start | bytes 776 | tf_op jit(solution)/shard_map/ppermute | solution.py:324
  6.0 5.6 %collective-permute-start = (s32[4,16]{1,0:T(4,128)}, s32[4,16]{1,0:T(4,128)S(1)}, u32[]{:S(2)}, u32[]{:S(2)}) collective-permute-start(s32[4,16]{1,0:T(4,128)} %bitcast.33), channel_id=1, source_target_pairs={{0,20},{1,21},{2,22},{3,23},{4,16},{5,17},{6,18},{7,19},{8,28},{9,... | collective-permute-start | bytes 776 | tf_op jit(solution)/shard_map/ppermute | solution.py:324
  8.0 0.7 copy-start.1
  8.7 0.7 copy-start.2
  11.6 4.4 %copy-start = (bf16[1,1,16,32,128]{4,3,2,1,0:T(8,128)(2,1)S(1)}, bf16[1,1,16,32,128]{4,3,2,1,0:T(8,128)(2,1)}, u32[]{:S(2)}) copy-start(bf16[1,1,16,32,128]{4,3,2,1,0:T(8,128)(2,1)} %param.6) | copy-start | bytes 393220
  11.6 4.4 %copy-start.3 = (f32[1,1,16,4]{2,3,1,0:T(4,128)S(1)}, f32[1,1,16,4]{2,3,1,0:T(4,128)}, u32[]{:S(2)}) copy-start(f32[1,1,16,4]{2,3,1,0:T(4,128)} %param.7) | copy-start | bytes 772
  14.0 32.3 %collective-permute-start.7 = (bf16[1040,128]{1,0:T(8,128)(2,1)}, bf16[1040,128]{1,0:T(8,128)(2,1)}, u32[]{:S(2)}, u32[]{:S(2)}) collective-permute-start(bf16[1040,128]{1,0:T(8,128)(2,1)} %get-tuple-element.29.after.refs_0_), channel_id=1, source_target_pairs={{0,4},{1,5},{2,6},{3,7},{4,0},{5,1},{6,2},{7,3},{8,12},{9,13},{10,... | collective-permute-start | bytes 798728 | tf_op jit(solution)/shard_map/ppermute | solution.py:315
  16.6 4.3 %collective-permute-start.3 = (bf16[272,128]{1,0:T(8,128)(2,1)S(1)}, bf16[272,128]{1,0:T(8,128)(2,1)S(1)}, u32[]{:S(2)}, u32[]{:S(2)}) collective-permute-start(bf16[272,128]{1,0:T(8,128)(2,1)S(1)} %get-tuple-element.31), channel_id=1, source_target_pairs={{0,1},{1,0},{2,3},{3,2},{4,5},{5,4},{6,7},{7,6},{8,9},{9,8},{10,11... | collective-permute-start | bytes 208904 | tf_op jit(solution)/shard_map/ppermute | solution.py:315
  19.2 41.0 %collective-permute-start.12 = (bf16[1040,128]{1,0:T(8,128)(2,1)}, bf16[1040,128]{1,0:T(8,128)(2,1)}, u32[]{:S(2)}, u32[]{:S(2)}) collective-permute-start(bf16[1040,128]{1,0:T(8,128)(2,1)} %get-tuple-element.33.refs_0_), channel_id=1, source_target_pairs={{0,2},{1,3},{2,4},{3,5},{4,6},{5,7},{6,0},{7,1},{8,10},{9,11},{10,... | collective-permute-start | bytes 798728 | tf_op jit(solution)/shard_map/ppermute | solution.py:315
  20.9 1.5 %copy-start.4 = (s32[1,1,16,4]{2,3,1,0:T(4,128)S(1)}, s32[1,1,16,4]{2,3,1,0:T(4,128)}, u32[]{:S(2)}) copy-start(s32[1,1,16,4]{2,3,1,0:T(4,128)} %param.8) | copy-start | bytes 772
  20.9 6.7 %collective-permute-start.4 = (bf16[1,2,272,128]{3,2,1,0:T(8,128)(2,1)S(1)}, bf16[1,2,272,128]{3,2,1,0:T(8,128)(2,1)S(1)}, u32[]{:S(2)}, u32[]{:S(2)}) collective-permute-start(bf16[1,2,272,128]{3,2,1,0:T(8,128)(2,1)S(1)} %bitcast.23), channel_id=1, source_target_pairs={{0,8},{8,0},{16,24},{24,16},{1,9},{9,1},{17,25},{25,17},{2,10},{10... | collective-permute-start | bytes 417800 | tf_op jit(solution)/shard_map/ppermute | solution.py:346
  24.1 26.8 %collective-permute-start.6 = (bf16[1040,128]{1,0:T(8,128)(2,1)S(1)}, bf16[1040,128]{1,0:T(8,128)(2,1)S(1)}, u32[]{:S(2)}, u32[]{:S(2)}) collective-permute-start(bf16[1040,128]{1,0:T(8,128)(2,1)S(1)} %get-tuple-element.32), channel_id=1, source_target_pairs={{0,5},{1,4},{2,7},{3,6},{4,1},{5,0},{6,3},{7,2},{8,13},{9,12},{10,... | collective-permute-start | bytes 798728 | tf_op jit(solution)/shard_map/ppermute | solution.py:315
  25.4 38.5 %collective-permute-start.11 = (bf16[1040,128]{1,0:T(8,128)(2,1)}, bf16[1040,128]{1,0:T(8,128)(2,1)}, u32[]{:S(2)}, u32[]{:S(2)}) collective-permute-start(bf16[1040,128]{1,0:T(8,128)(2,1)} %get-tuple-element.41), channel_id=1, source_target_pairs={{0,3},{1,2},{2,5},{3,4},{4,7},{5,6},{6,1},{7,0},{8,11},{9,10},{10,... | collective-permute-start | bytes 798728 | tf_op jit(solution)/shard_map/ppermute | solution.py:315
  27.6 8.6 %collective-permute-start.5 = (bf16[2,2,272,128]{3,2,1,0:T(8,128)(2,1)S(1)}, bf16[2,2,272,128]{3,2,1,0:T(8,128)(2,1)S(1)}, u32[]{:S(2)}, u32[]{:S(2)}) collective-permute-start(bf16[2,2,272,128]{3,2,1,0:T(8,128)(2,1)S(1)} %join.4.own), channel_id=1, source_target_pairs={{0,16},{8,24},{16,0},{24,8},{1,17},{9,25},{17,1},{25,9},{2,18},{10... | collective-permute-start | bytes 835592 | tf_op jit(solution)/shard_map/ppermute | solution.py:346
  36.2 19.0 %collective-permute-start.13 = (bf16[1040,128]{1,0:T(8,128)(2,1)S(1)}, bf16[1040,128]{1,0:T(8,128)(2,1)S(1)}, u32[]{:S(2)}, u32[]{:S(2)}) collective-permute-start(bf16[1040,128]{1,0:T(8,128)(2,1)S(1)} %get-tuple-element.42), channel_id=1, source_target_pairs={{0,1},{1,0},{2,3},{3,2},{4,5},{5,4},{6,7},{7,6},{8,9},{9,8},{10,11... | collective-permute-start | bytes 798728 | tf_op jit(solution)/shard_map/ppermute | solution.py:315
  46.3 21.2 %collective-permute-start.10 = (bf16[1040,128]{1,0:T(8,128)(2,1)S(1)}, bf16[1040,128]{1,0:T(8,128)(2,1)S(1)}, u32[]{:S(2)}, u32[]{:S(2)}) collective-permute-start(bf16[1040,128]{1,0:T(8,128)(2,1)S(1)} %gather_rows.9.refs_3_), channel_id=1, source_target_pairs={{0,6},{1,7},{2,0},{3,1},{4,2},{5,3},{6,4},{7,5},{8,14},{9,15},{10,... | collective-permute-start | bytes 798728 | tf_op jit(solution)/shard_map/ppermute | solution.py:315
  50.9 19.9 %collective-permute-start.9 = (bf16[784,128]{1,0:T(8,128)(2,1)S(1)}, bf16[784,128]{1,0:T(8,128)(2,1)S(1)}, u32[]{:S(2)}, u32[]{:S(2)}) collective-permute-start(bf16[784,128]{1,0:T(8,128)(2,1)S(1)} %gather_rows.10.refs_3_), channel_id=1, source_target_pairs={{0,7},{1,6},{2,1},{3,0},{4,3},{5,2},{6,5},{7,4},{8,15},{9,14},{10,... | collective-permute-start | bytes 602120 | tf_op jit(solution)/shard_map/ppermute | solution.py:315
  55.2 22.2 %collective-permute-start.8 = (bf16[272,128]{1,0:T(8,128)(2,1)S(1)}, bf16[272,128]{1,0:T(8,128)(2,1)S(1)}, u32[]{:S(2)}, u32[]{:S(2)}) collective-permute-start(bf16[272,128]{1,0:T(8,128)(2,1)S(1)} %gather_rows.11), channel_id=1, source_target_pairs={{0,7},{1,6},{2,1},{3,0},{4,3},{5,2},{6,5},{7,4},{8,15},{9,14},{10,... | collective-permute-start | bytes 208904 | tf_op jit(solution)/shard_map/ppermute | solution.py:315
